TPU v7x, 32 devices: a whole 2x2x4 slice. The times are simulated.
32 devices in a mesh: dp: 8 (over y, x, core), seq: 4 (over z).
Axes of the slice: x: 2, y: 2, z: 4, core: 2. Of those that a mesh axis runs over, the one named last changes fastest.
Arguments:
- inputs: bfloat16 [2, 8, 1024, 2048], P(None, 'dp', 'seq'), may hold values from -6 to 6
- cotangent: bfloat16 [2, 8, 1024, 2048], P(None, 'dp', 'seq'), may hold values from -6 to 6
- doc_ids: int32 [2, 8, 1024], P(None, 'dp', 'seq'), may hold values from 0 to 4, as said below
- valid_mask: int32 [2, 8, 1024], P(None, 'dp', 'seq'), may hold values 0 or 1
- gain_attn: bfloat16 [2048], P(('dp', 'seq')), may hold values from 0.5 to 1.5
- w_query: bfloat16 [2048, 2048], P(('dp', 'seq')), may hold values from -0.125 to 0.125
- w_key: bfloat16 [2048, 2048], P(('dp', 'seq')), may hold values from -0.125 to 0.125
- w_value: bfloat16 [2048, 2048], P(('dp', 'seq')), may hold values from -0.125 to 0.125
- w_out: bfloat16 [2048, 2048], P(('dp', 'seq')), may hold values from -1 to 1
- gain_mlp: bfloat16 [2048], P(('dp', 'seq')), may hold values from 0.5 to 1.5
- w_gate: bfloat16 [2048, 8192], P(('dp', 'seq')), may hold values from -0.125 to 0.125
- w_up: bfloat16 [2048, 8192], P(('dp', 'seq')), may hold values from -0.125 to 0.125
- w_down: bfloat16 [8192, 2048], P(('dp', 'seq')), may hold values from -0.0625 to 0.0625
Outputs:
- output: bfloat16 [2, 8, 1024, 2048], P(None, 'dp', 'seq')
- grad_input: bfloat16 [2, 8, 1024, 2048], P(None, 'dp', 'seq')
- grad_gain_attn: float32 [2048], P(('dp', 'seq'))
- grad_query: float32 [2048, 2048], P(('dp', 'seq'))
- grad_key: float32 [2048, 2048], P(('dp', 'seq'))
- grad_value: float32 [2048, 2048], P(('dp', 'seq'))
- grad_out: float32 [2048, 2048], P(('dp', 'seq'))
- grad_gain_mlp: float32 [2048], P(('dp', 'seq'))
- grad_gate: float32 [2048, 8192], P(('dp', 'seq'))
- grad_up: float32 [2048, 8192], P(('dp', 'seq'))
- grad_down: float32 [8192, 2048], P(('dp', 'seq'))
Inputs may be any that keep to these rules, and one draw needn't show every extreme that they name: `doc_ids`: document ids along a row start at 0 and never fall; tokens with one id form one document; every row reaches id 4.
All inputs are finite; a program needn't handle non-finite values. No bound on the sum of `valid_mask` on one device may be relied on, other than what follows from the above.
Results may differ from a plain program's by a relative error of at most 0.015.
Values may be sent and summed in bfloat16 or wider, within the bound.
No kernel may reach another device: no remote copies, remote signals or barrier semaphores. Data moves between devices by JAX's collectives and lax.ppermute only.
A program may use at most 768 MiB of HBM per device.

v0:
```python
import jax
import jax.numpy as jnp
from jax import lax
from jax.sharding import PartitionSpec as P

HD = 64


NORM_EPS = 1e-05
ROPE_BASE = 130000.0
MASK_FILL = -1e30


def contract_last(left, right):
    return lax.dot_general(
        left, right, (((1,), (1,)), ((), ())), preferred_element_type=jnp.float32
    )


def contract_first(left, right):
    return lax.dot_general(
        left, right, (((0,), (0,)), ((), ())), preferred_element_type=jnp.float32
    )


def norm_scale(values):
    return lax.rsqrt(jnp.mean(values * values, axis=-1, keepdims=True) + NORM_EPS)


def norm_back(grad_normed, values, scale_rows, gain):
    unit = values * scale_rows
    scaled = grad_normed * gain
    grad_values = scale_rows * (scaled - unit * jnp.mean(scaled * unit, axis=-1, keepdims=True))
    return (grad_values, jnp.sum(grad_normed * unit, axis=0))


def rope_tables(positions, head_dim):
    exponent = jnp.arange(head_dim // 2, dtype=jnp.float32) * (2.0 / head_dim)
    inverse = jnp.power(ROPE_BASE, -exponent)
    angles = positions.astype(jnp.float32)[:, None] * inverse[None, :]
    return (jnp.cos(angles)[:, None, :], jnp.sin(angles)[:, None, :])


def rotate(field_in, cosine_table, sine_table):
    half_width = field_in.shape[-1] // 2
    front_half = field_in[..., :half_width]
    back_half = field_in[..., half_width:]
    return jnp.concatenate(
        [
            front_half * cosine_table - back_half * sine_table,
            back_half * cosine_table + front_half * sine_table,
        ],
        axis=-1,
    )


def unrotate(field_in, cosine_table, sine_table):
    half_width = field_in.shape[-1] // 2
    front_half = field_in[..., :half_width]
    back_half = field_in[..., half_width:]
    return jnp.concatenate(
        [
            front_half * cosine_table + back_half * sine_table,
            back_half * cosine_table - front_half * sine_table,
        ],
        axis=-1,
    )


def send_grads(
    normed,
    attn_grads,
    attended,
    grad_branch,
    normed_mlp,
    mlp_grads,
    activated,
    grad_result_low,
    gain_attn_term,
    gain_mlp_term,
):
    wide_shard = lax.psum_scatter(
        jnp.concatenate(
            [
                contract_first(normed, attn_grads),
                contract_first(attended, grad_branch),
                contract_first(normed_mlp, mlp_grads),
            ],
            axis=1,
        ),
        ("dp", "seq"),
        scatter_dimension=0,
        tiled=True,
    )
    down_total = contract_first(activated, grad_result_low)
    down_shard, gain_attn_shard, gain_mlp_shard = (
        lax.psum_scatter(down_total, ("dp", "seq"), scatter_dimension=0, tiled=True),
        lax.psum_scatter(gain_attn_term, ("dp", "seq"), scatter_dimension=0, tiled=True),
        lax.psum_scatter(gain_mlp_term, ("dp", "seq"), scatter_dimension=0, tiled=True),
    )
    return (wide_shard, down_shard, gain_attn_shard, gain_mlp_shard)


def on_device(
    inputs,
    cotangent,
    doc_ids,
    valid_mask,
    gain_attn,
    w_query,
    w_key,
    w_value,
    w_out,
    gain_mlp,
    w_gate,
    w_up,
    w_down,
):
    micro_count = inputs.shape[0]
    tokens = inputs.shape[2]
    model_width = inputs.shape[3]
    head_dim = HD
    head_count = model_width // head_dim
    hidden_units = w_gate.shape[1]
    score_scale = float(head_dim) ** (-0.5)
    all_rows = micro_count * tokens
    seq_rank = lax.axis_index("seq")
    local_pos = seq_rank * tokens + jnp.arange(tokens, dtype=jnp.int32)
    attn_set = (
        lax.all_gather(gain_attn, ("dp", "seq"), axis=0, tiled=True),
        lax.all_gather(w_query, ("dp", "seq"), axis=0, tiled=True),
        lax.all_gather(w_key, ("dp", "seq"), axis=0, tiled=True),
        lax.all_gather(w_value, ("dp", "seq"), axis=0, tiled=True),
        lax.all_gather(w_out, ("dp", "seq"), axis=0, tiled=True),
    )
    hidden_in = inputs[:, 0].reshape(all_rows, model_width).astype(jnp.float32)
    scale_in = norm_scale(hidden_in)
    normed = (hidden_in * scale_in * attn_set[0]).astype(jnp.bfloat16)
    local_doc = doc_ids[:, 0]
    row_doc, row_valid = (
        lax.all_gather(local_doc, "seq", axis=1, tiled=True),
        lax.all_gather(valid_mask[:, 0], "seq", axis=1, tiled=True),
    )
    before = jnp.sum((row_doc[:, None, :] < local_doc[:, :, None]).astype(jnp.int32), axis=2)
    positions = (local_pos[None, :] - before).reshape(all_rows)
    cosine_table, sine_table = rope_tables(positions, head_dim)
    query_raw = jnp.dot(normed, attn_set[1], preferred_element_type=jnp.float32).reshape(
        all_rows, head_count, head_dim
    )
    key_raw = jnp.dot(normed, attn_set[2], preferred_element_type=jnp.float32).reshape(
        all_rows, head_count, head_dim
    )
    value_raw = jnp.dot(normed, attn_set[3], preferred_element_type=jnp.float32)
    queries = rotate(query_raw, cosine_table, sine_table).astype(jnp.bfloat16)
    keys_local = (
        rotate(key_raw, cosine_table, sine_table)
        .astype(jnp.bfloat16)
        .reshape(micro_count, tokens, head_count, head_dim)
    )
    values_local = value_raw.astype(jnp.bfloat16).reshape(micro_count, tokens, head_count, head_dim)
    all_keys, all_values = (
        lax.all_gather(keys_local, "seq", axis=1, tiled=True),
        lax.all_gather(values_local, "seq", axis=1, tiled=True),
    )
    length = all_keys.shape[1]
    key_pos = jnp.arange(length, dtype=jnp.int32)
    masks = []
    log_totals = []
    attended_parts = []
    for micro_step in range(micro_count):
        allowed = (row_doc[micro_step][None, :] == local_doc[micro_step][:, None]) & (
            key_pos[None, :] <= local_pos[:, None]
        )
        allowed = (
            allowed
            & ((row_valid[micro_step][None, :] == 1) | (key_pos[None, :] == local_pos[:, None]))
        )[None]
        query_rows = queries[micro_step * tokens : (micro_step + 1) * tokens]
        scores = (
            jnp.einsum(
                "thd,jhd->htj", query_rows, all_keys[micro_step], preferred_element_type=jnp.float32
            )
            * score_scale
        )
        row_top = jnp.max(jnp.where(allowed, scores, MASK_FILL), axis=-1, keepdims=True)
        exp_scores = jnp.where(allowed, jnp.exp(scores - row_top), 0.0)
        row_total = jnp.sum(exp_scores, axis=-1, keepdims=True)
        probs_low = (exp_scores / row_total).astype(jnp.bfloat16)
        masks.append(allowed)
        log_totals.append(row_top + jnp.log(row_total))
        mixed = jnp.einsum(
            "htj,jhd->thd", probs_low, all_values[micro_step], preferred_element_type=jnp.float32
        )
        attended_parts.append(mixed.reshape(tokens, model_width))
    attended = jnp.concatenate(attended_parts, axis=0).astype(jnp.bfloat16)
    middle = hidden_in + jnp.dot(attended, attn_set[4], preferred_element_type=jnp.float32)
    mlp_set = (
        lax.all_gather(gain_mlp, ("dp", "seq"), axis=0, tiled=True),
        lax.all_gather(w_gate, ("dp", "seq"), axis=0, tiled=True),
        lax.all_gather(w_up, ("dp", "seq"), axis=0, tiled=True),
        lax.all_gather(w_down, ("dp", "seq"), axis=0, tiled=True),
    )
    scale_mid = norm_scale(middle)
    normed_mlp = (middle * scale_mid * mlp_set[0]).astype(jnp.bfloat16)
    gate_proj = jnp.dot(normed_mlp, mlp_set[1], preferred_element_type=jnp.float32)
    up_proj = jnp.dot(normed_mlp, mlp_set[2], preferred_element_type=jnp.float32)
    sigmoid_gate = jax.nn.sigmoid(gate_proj)
    silu_gate = gate_proj * sigmoid_gate
    activated = (silu_gate * up_proj).astype(jnp.bfloat16)
    result = middle + jnp.dot(activated, mlp_set[3], preferred_element_type=jnp.float32)
    output = result.astype(jnp.bfloat16).reshape(micro_count, 1, tokens, model_width)
    attn_back = (
        lax.all_gather(gain_attn, ("dp", "seq"), axis=0, tiled=True),
        lax.all_gather(w_query, ("dp", "seq"), axis=0, tiled=True),
        lax.all_gather(w_key, ("dp", "seq"), axis=0, tiled=True),
        lax.all_gather(w_value, ("dp", "seq"), axis=0, tiled=True),
        lax.all_gather(w_out, ("dp", "seq"), axis=0, tiled=True),
    )
    mlp_back = (
        lax.all_gather(gain_mlp, ("dp", "seq"), axis=0, tiled=True),
        lax.all_gather(w_gate, ("dp", "seq"), axis=0, tiled=True),
        lax.all_gather(w_up, ("dp", "seq"), axis=0, tiled=True),
        lax.all_gather(w_down, ("dp", "seq"), axis=0, tiled=True),
    )
    grad_result_low = cotangent[:, 0].reshape(all_rows, model_width)
    grad_result = grad_result_low.astype(jnp.float32)
    grad_activated = contract_last(grad_result_low, mlp_back[3])
    grad_gate = (
        grad_activated * up_proj * sigmoid_gate * (1.0 + gate_proj * (1.0 - sigmoid_gate))
    ).astype(jnp.bfloat16)
    grad_up = (grad_activated * silu_gate).astype(jnp.bfloat16)
    grad_normed_mlp = contract_last(grad_gate, mlp_back[1]) + contract_last(grad_up, mlp_back[2])
    grad_mid_norm, gain_mlp_term = norm_back(grad_normed_mlp, middle, scale_mid, mlp_back[0])
    grad_middle = grad_result + grad_mid_norm
    grad_branch = grad_middle.astype(jnp.bfloat16)
    grad_attended = (
        contract_last(grad_branch, attn_back[4])
        .astype(jnp.bfloat16)
        .reshape(all_rows, head_count, head_dim)
    )
    query_grad_parts = []
    key_grad_parts = []
    value_grad_parts = []
    for micro_step in range(micro_count):
        query_rows = queries[micro_step * tokens : (micro_step + 1) * tokens]
        attended_grad_rows = grad_attended[micro_step * tokens : (micro_step + 1) * tokens]
        allowed = masks[micro_step]
        scores = (
            jnp.einsum(
                "thd,jhd->htj", query_rows, all_keys[micro_step], preferred_element_type=jnp.float32
            )
            * score_scale
        )
        probs_again = jnp.where(allowed, jnp.exp(scores - log_totals[micro_step]), 0.0)
        grad_probs = jnp.einsum(
            "thd,jhd->htj",
            attended_grad_rows,
            all_values[micro_step],
            preferred_element_type=jnp.float32,
        )
        grad_scores = (
            probs_again * (grad_probs - jnp.sum(grad_probs * probs_again, axis=-1, keepdims=True))
        ).astype(jnp.bfloat16)
        query_grad_parts.append(
            jnp.einsum(
                "htj,jhd->thd",
                grad_scores,
                all_keys[micro_step],
                preferred_element_type=jnp.float32,
            )
            * score_scale
        )
        key_grad_parts.append(
            jnp.einsum("htj,thd->jhd", grad_scores, query_rows, preferred_element_type=jnp.float32)
            * score_scale
        )
        value_grad_parts.append(
            jnp.einsum(
                "htj,thd->jhd",
                probs_again.astype(jnp.bfloat16),
                attended_grad_rows,
                preferred_element_type=jnp.float32,
            )
        )
    grad_queries = jnp.concatenate(query_grad_parts, axis=0)
    grad_keys_local, grad_values_local = (
        lax.psum_scatter(
            jnp.stack(key_grad_parts).astype(jnp.bfloat16), "seq", scatter_dimension=1, tiled=True
        ).astype(jnp.float32),
        lax.psum_scatter(
            jnp.stack(value_grad_parts).astype(jnp.bfloat16), "seq", scatter_dimension=1, tiled=True
        ).astype(jnp.float32),
    )
    grad_query_raw = (
        unrotate(grad_queries, cosine_table, sine_table)
        .reshape(all_rows, model_width)
        .astype(jnp.bfloat16)
    )
    grad_key_raw = (
        unrotate(grad_keys_local.reshape(all_rows, head_count, head_dim), cosine_table, sine_table)
        .reshape(all_rows, model_width)
        .astype(jnp.bfloat16)
    )
    grad_value_raw = grad_values_local.reshape(all_rows, model_width).astype(jnp.bfloat16)
    grad_normed = (
        contract_last(grad_query_raw, attn_back[1])
        + contract_last(grad_key_raw, attn_back[2])
        + contract_last(grad_value_raw, attn_back[3])
    )
    grad_in_norm, gain_attn_term = norm_back(grad_normed, hidden_in, scale_in, attn_back[0])
    grad_input = (
        (grad_middle + grad_in_norm)
        .astype(jnp.bfloat16)
        .reshape(micro_count, 1, tokens, model_width)
    )
    attn_grads = jnp.concatenate([grad_query_raw, grad_key_raw, grad_value_raw], axis=1)
    mlp_grads = jnp.concatenate([grad_gate, grad_up], axis=1)
    wide_shard, down_shard, gain_attn_shard, gain_mlp_shard = send_grads(
        normed,
        attn_grads,
        attended,
        grad_branch,
        normed_mlp,
        mlp_grads,
        activated,
        grad_result_low,
        gain_attn_term,
        gain_mlp_term,
    )
    grad_query = wide_shard[:, 0:model_width]
    grad_key = wide_shard[:, model_width : 2 * model_width]
    grad_value = wide_shard[:, 2 * model_width : 3 * model_width]
    grad_out = wide_shard[:, 3 * model_width : 4 * model_width]
    grad_gate_shard = wide_shard[:, 4 * model_width : 4 * model_width + hidden_units]
    grad_up_shard = wide_shard[:, 4 * model_width + hidden_units :]
    return (
        output,
        grad_input,
        gain_attn_shard,
        grad_query,
        grad_key,
        grad_value,
        grad_out,
        gain_mlp_shard,
        grad_gate_shard,
        grad_up_shard,
        down_shard,
    )


def solution(mesh):
    placed = (
        P(None, "dp", "seq", None),
        P(None, "dp", "seq", None),
        P(None, "dp", "seq"),
        P(None, "dp", "seq"),
        P(("dp", "seq")),
        P(("dp", "seq"), None),
        P(("dp", "seq"), None),
        P(("dp", "seq"), None),
        P(("dp", "seq"), None),
        P(("dp", "seq")),
        P(("dp", "seq"), None),
        P(("dp", "seq"), None),
        P(("dp", "seq"), None),
    )
    return jax.shard_map(
        on_device,
        mesh=mesh,
        in_specs=placed,
        out_specs=(
            P(None, "dp", "seq", None),
            P(None, "dp", "seq", None),
            P(("dp", "seq")),
            P(("dp", "seq"), None),
            P(("dp", "seq"), None),
            P(("dp", "seq"), None),
            P(("dp", "seq"), None),
            P(("dp", "seq")),
            P(("dp", "seq"), None),
            P(("dp", "seq"), None),
            P(("dp", "seq"), None),
        ),
        check_vma=False,
    )
```

profile of v0, /device:TPU:0, one launch (start us, length us, event | category | flops | bytes accessed | tf_op | source)
XLA Modules:
  0.0 4834.7 jit_solution(11977688144743636950)
XLA Ops:
  11.8 42.8 all-reduce.5
  54.6 10.3 all-gather
  69.6 21.8 all-gather.18.cloned.1.call-done
  91.4 12.3 copy.66
  103.7 66.7 %all-gather.16.cloned.1.call-done = bf16[2048,2048]{1,0:T(8,128)(2,1)} async-done(((bf16[64,2048]{1,0:T(8,128)(2,1)}), bf16[2048,2048]{1,0:T(8,128)(2,1)}) %all-gather.16.cloned.1.call-update) | async-done | bytes 8388624 | tf_op jit(solution)/shard_map/all_gather | solution.py:131
  170.4 12.3 copy.65
  201.6 47.7 all-gather.12.cloned.1.call-done
  249.3 8.5 convolution_convert_fusion.1
  272.5 9.7 all-gather.1
  283.0 116.1 %all-gather.20.cloned.1.call-done = bf16[2,1024,32,64]{1,3,2,0:T(8,128)(2,1)} async-done(((bf16[2,256,32,64]{1,3,2,0:T(8,128)(2,1)}), bf16[2,1024,32,64]{1,3,2,0:T(8,128)(2,1)}) %all-gather.20.cloned.1.call-update) | async-done | bytes 8388624 | tf_op jit(solution)/shard_map/all_gather | solution.py:162
  399.1 18.1 select_reduce_fusion
  417.2 16.1 select_reduce_fusion.1
  433.3 16.1 fusion.1
  453.8 9.3 fusion
  463.1 85.4 %all-gather.14.cloned.1.call-done = bf16[2,1024,32,64]{1,3,2,0:T(8,128)(2,1)} async-done(((bf16[2,256,32,64]{1,3,2,0:T(8,128)(2,1)}), bf16[2,1024,32,64]{1,3,2,0:T(8,128)(2,1)}) %all-gather.14.cloned.1.call-update) | async-done | bytes 8388624 | tf_op jit(solution)/shard_map/all_gather | solution.py:163
  548.5 17.1 fusion.50
  565.6 15.6 fusion.51
  581.2 45.6 all-gather.22.cloned.1.call-done
  637.0 186.1 %all-gather.26.cloned.1.call-done = bf16[2048,8192]{1,0:T(8,128)(2,1)} async-done(((bf16[64,8192]{1,0:T(8,128)(2,1)}), bf16[2048,8192]{1,0:T(8,128)(2,1)}) %all-gather.26.cloned.1.call-update) | async-done | bytes 33554448 | tf_op jit(solution)/shard_map/all_gather | solution.py:200
  823.2 26.6 fusion.87
  849.8 169.3 %all-gather.24.cloned.1.call-done = bf16[2048,8192]{1,0:T(8,128)(2,1)} async-done(((bf16[64,8192]{1,0:T(8,128)(2,1)}), bf16[2048,8192]{1,0:T(8,128)(2,1)}) %all-gather.24.cloned.1.call-update) | async-done | bytes 33554448 | tf_op jit(solution)/shard_map/all_gather | solution.py:199
  1019.1 26.9 fusion.86
  1045.9 169.1 %all-gather.28.cloned.1.call-done = bf16[8192,2048]{1,0:T(8,128)(2,1)} async-done(((bf16[256,2048]{1,0:T(8,128)(2,1)}), bf16[8192,2048]{1,0:T(8,128)(2,1)}) %all-gather.28.cloned.1.call-update) | async-done | bytes 33554448 | tf_op jit(solution)/shard_map/all_gather | solution.py:201
  1215.0 38.6 multiply_convert_fusion.2
  1253.7 25.6 fusion.88
  1279.3 26.7 multiply_reduce_fusion.2
  1310.0 9.7 convolution_convert_fusion
  1322.9 16.3 convert_bitcast_fusion.1
  1339.3 16.1 convert_bitcast_fusion.2
  1362.9 26.9 multiply_reduce_fusion.1
  1389.7 26.6 multiply_reduce_fusion
  1416.4 57.0 %multiply_convert_fusion = (bf16[32,256,1024]{2,1,0:T(8,128)(2,1)}, bf16[32,256,1024]{2,1,0:T(8,128)(2,1)}) fusion(f32[32,256,1024]{2,1,0:T(8,128)} %get-tuple-element.106, f32[32,256,1024]{2,1,0:T(8,128)} %get-tuple-element.99, f32[32,256]{1,0:T(8,128)S(1)} %get-tuple-element.105, f32[32,256]{1,0:T(8,128)S(1)} %copy-done.27, ...), kind=kLoop, calls=%fused_computation.1 | loop fusion | flops 100663296 | bytes 168427520 | tf_op jit(solution)/shard_map/convert_element_type | solution.py:263
  1473.5 11.2 fusion.24
  1499.8 11.0 fusion.52
  1510.8 11.6 multiply_bitcast_fusion
  1522.4 10.4 multiply_bitcast_fusion.1
  1532.8 55.2 %fusion.4 = f32[2048,16384]{1,0:T(8,128)} fusion(bf16[512,2048]{1,0:T(8,128)(2,1)S(1)} %copy-done.11, bf16[512,8192]{1,0:T(8,128)(2,1)} %get-tuple-element.65, bf16[512,8192]{1,0:T(8,128)(2,1)} %get-tuple-element.66), kind=kOutput, calls=%fused_computation.17 | convolution fusion | flops 34393292800 | bytes 153092096 | tf_op jit(solution)/shard_map/dot_general | solution.py:21
  1593.6 59.6 %reduce-scatter.5.cloned.1.call-done = bf16[2,256,32,64]{1,3,2,0:T(8,128)(2,1)} async-done(((bf16[2,1024,32,64]{1,3,2,0:T(8,128)(2,1)}), bf16[2,256,32,64]{1,3,2,0:T(8,128)(2,1)}) %reduce-scatter.5.cloned.1.call-update) | async-done | bytes 2097168 | tf_op jit(solution)/shard_map/reduce_scatter | solution.py:287
  1661.2 23.8 fusion.17
  1685.1 130.6 %pad_maximum_fusion = f32[2048,24576]{1,0:T(8,128)} fusion(f32[2048,16384]{1,0:T(8,128)} %fusion.4, f32[2048,2048]{1,0:T(8,128)} %fusion.52, f32[2048,6144]{1,0:T(8,128)} %fusion.17), kind=kLoop, calls=%fused_computation | loop fusion | flops 100663296 | bytes 402653184 | tf_op jit(solution)/shard_map/concatenate | solution.py:83
  1817.3 44.9 fusion.91
  1862.2 30.0 add_convert_fusion
  1892.3 8.1 fusion.90
  1900.4 11.5 fusion.89
  1912.0 13.6 fusion.35
  1925.6 41.3 all-reduce.4
  1975.6 1439.6 %reduce-scatter.9.cloned.1.call-done = f32[64,24576]{1,0:T(8,128)} async-done(((f32[2048,24576]{1,0:T(8,128)}), f32[64,24576]{1,0:T(8,128)}) %reduce-scatter.9.cloned.1.call-update) | async-done | bytes 6291472 | tf_op jit(solution)/shard_map/reduce_scatter | solution.py:82
  3422.7 1405.1 %reduce-scatter.11.cloned.1.call-done = f32[256,2048]{1,0:T(8,128)} async-done(((f32[8192,2048]{1,0:T(8,128)}), f32[256,2048]{1,0:T(8,128)}) %reduce-scatter.11.cloned.1.call-update) | async-done | bytes 2097168 | tf_op jit(solution)/shard_map/reduce_scatter | solution.py:97
  (181 shorter events, 119.3 us)
Async XLA Ops:
  7.2 60.6 %copy-start.2 = (bf16[2,1,256,2048]{3,2,1,0:T(8,128)(2,1)S(1)}, bf16[2,1,256,2048]{3,2,1,0:T(8,128)(2,1)}, u32[]{:S(2)}) copy-start(bf16[2,1,256,2048]{3,2,1,0:T(8,128)(2,1)} %param.13) | copy-start | bytes 6291460
  7.2 84.3 %all-gather.18.cloned.1.call-start = ((), (), s32[]{:S(2)}) async-start(), calls=%async_computation.7 | async-start | bytes 8650752 | tf_op jit(solution)/shard_map/all_gather | solution.py:132
  7.9 162.5 %all-gather.16.cloned.1.call-start = ((), (), s32[]{:S(2)}) async-start(), calls=%async_computation.6 | async-start | bytes 8650752 | tf_op jit(solution)/shard_map/all_gather | solution.py:131
  8.7 240.6 %all-gather.12.cloned.1.call-start = ((), (), s32[]{:S(2)}) async-start(), calls=%async_computation.4 | async-start | bytes 8650752 | tf_op jit(solution)/shard_map/all_gather | solution.py:133
  9.4 389.7 %all-gather.20.cloned.1.call-start = ((), (), s32[]{:S(2)}) async-start(), calls=%async_computation.8 | async-start | bytes 10485760 | tf_op jit(solution)/shard_map/all_gather | solution.py:162
  54.6 145.1 %copy-start.33 = (f32[2048]{0:T(1024)}, f32[2048]{0:T(1024)S(1)}, u32[]{:S(2)}) copy-start(f32[2048]{0:T(1024)S(1)} %convert_element_type.112) | copy-start | bytes 24580
  67.7 127.4 %copy-start.29 = (f32[512,32]{0,1:T(8,128)}, f32[512,32]{0,1:T(8,128)S(1)}, u32[]{:S(2)}) copy-start(f32[512,32]{0,1:T(8,128)S(1)} %get-tuple-element.90) | copy-start | bytes 196612
  67.7 127.4 %copy-start.31 = (f32[512,32]{0,1:T(8,128)}, f32[512,32]{0,1:T(8,128)S(1)}, u32[]{:S(2)}) copy-start(f32[512,32]{0,1:T(8,128)S(1)} %get-tuple-element.91) | copy-start | bytes 196612
  197.6 219.6 %copy-start.5 = (bf16[512,32,32]{0,2,1:T(8,128)(2,1)}, bf16[512,32,32]{0,2,1:T(8,128)(2,1)S(1)}, u32[]{:S(2)}) copy-start(bf16[512,32,32]{0,2,1:T(8,128)(2,1)S(1)} %get-tuple-element.78) | copy-start | bytes 3145732
  199.5 349.0 %all-gather.14.cloned.1.call-start = ((), (), s32[]{:S(2)}) async-start(), calls=%async_computation.5 | async-start | bytes 10485760 | tf_op jit(solution)/shard_map/all_gather | solution.py:163
  199.7 58.1 %copy-start.37 = (f32[1,2,2,128]{3,1,2,0:T(2,128)}, f32[1,2,2,128]{3,1,2,0:T(2,128)S(1)}, u32[]{:S(2)}) copy-start(f32[1,2,2,128]{3,1,2,0:T(2,128)S(1)} %copy.84) | copy-start | bytes 6148
  269.0 13.2 copy-start.39
  269.0 130.2 %copy-start.7 = (bf16[512,32,32]{0,2,1:T(8,128)(2,1)S(1)}, bf16[512,32,32]{0,2,1:T(8,128)(2,1)}, u32[]{:S(2)}) copy-start(bf16[512,32,32]{0,2,1:T(8,128)(2,1)} %get-tuple-element.79) | copy-start | bytes 3145732
  269.0 357.8 %all-gather.22.cloned.1.call-start = ((), (), s32[]{:S(2)}) async-start(), calls=%async_computation.9 | async-start | bytes 8650752 | tf_op jit(solution)/shard_map/all_gather | solution.py:134
  269.6 553.6 %all-gather.26.cloned.1.call-start = ((), (), s32[]{:S(2)}) async-start(), calls=%async_computation.11 | async-start | bytes 34603008 | tf_op jit(solution)/shard_map/all_gather | solution.py:200
  270.3 748.7 %all-gather.24.cloned.1.call-start = ((), (), s32[]{:S(2)}) async-start(), calls=%async_computation.10 | async-start | bytes 34603008 | tf_op jit(solution)/shard_map/all_gather | solution.py:199
  271.1 943.9 %all-gather.28.cloned.1.call-start = ((), (), s32[]{:S(2)}) async-start(), calls=%async_computation.12 | async-start | bytes 34603008 | tf_op jit(solution)/shard_map/all_gather | solution.py:201
  271.8 1316.1 %reduce-scatter.7.cloned.1.call-start = ((), (), s32[]{:S(2)}) async-start(), calls=%async_computation.14 | async-start | bytes 10485760 | tf_op jit(solution)/shard_map/reduce_scatter | solution.py:290
  283.0 265.5 %copy-start.18 = (pred[256,1024]{1,0:T(8,128)(4,1)}, pred[256,1024]{1,0:T(8,128)(4,1)S(1)}, u32[]{:S(2)}) copy-start(pred[256,1024]{1,0:T(8,128)(4,1)S(1)} %get-tuple-element.97) | copy-start | bytes 786436
  283.0 282.6 %copy-start.16 = (pred[256,1024]{1,0:T(8,128)(4,1)}, pred[256,1024]{1,0:T(8,128)(4,1)S(1)}, u32[]{:S(2)}) copy-start(pred[256,1024]{1,0:T(8,128)(4,1)S(1)} %get-tuple-element.96) | copy-start | bytes 786436
  433.3 20.5 copy-start
  548.5 17.1 copy-start.9
  565.6 61.2 %copy-start.3 = (bf16[2,1,256,2048]{3,2,1,0:T(8,128)(2,1)S(1)}, bf16[2,1,256,2048]{3,2,1,0:T(8,128)(2,1)}, u32[]{:S(2)}) copy-start(bf16[2,1,256,2048]{3,2,1,0:T(8,128)(2,1)} %param.13) | copy-start | bytes 6291460
  626.8 9.7 copy-start.35
  634.6 215.2 %copy-start.40 = (f32[512]{0:T(512)}, f32[512]{0:T(512)S(1)}, u32[]{:S(2)}) copy-start(f32[512]{0:T(512)S(1)} %add_rsqrt_fusion) | copy-start | bytes 6148
  637.0 382.1 %copy-start.10 = (bf16[512,2048]{1,0:T(8,128)(2,1)}, bf16[512,2048]{1,0:T(8,128)(2,1)S(1)}, u32[]{:S(2)}) copy-start(bf16[512,2048]{1,0:T(8,128)(2,1)S(1)} %multiply_convert_fusion.7) | copy-start | bytes 6291460
  1253.7 25.6 copy-start.14
  1253.7 25.6 copy-start.36
  1253.7 25.6 copy-start.41
  1310.0 9.8 copy-start.12
  1322.9 16.3 copy-start.17
  1322.9 16.3 copy-start.28
  1362.8 290.4 %reduce-scatter.5.cloned.1.call-start = ((), (), s32[]{:S(2)}) async-start(), calls=%async_computation.13 | async-start | bytes 10485760 | tf_op jit(solution)/shard_map/reduce_scatter | solution.py:287
  1416.4 57.1 %copy-start.6 = (bf16[512,32,32]{0,2,1:T(8,128)(2,1)S(1)}, bf16[512,32,32]{0,2,1:T(8,128)(2,1)}, u32[]{:S(2)}) copy-start(bf16[512,32,32]{0,2,1:T(8,128)(2,1)} %copy-done.5) | copy-start | bytes 3145732
  1416.4 57.1 %copy-start.8 = (bf16[512,32,32]{0,2,1:T(8,128)(2,1)S(1)}, bf16[512,32,32]{0,2,1:T(8,128)(2,1)}, u32[]{:S(2)}) copy-start(bf16[512,32,32]{0,2,1:T(8,128)(2,1)} %get-tuple-element.79) | copy-start | bytes 3145732
  1473.4 12.2 copy-start.1
  1498.3 1916.9 %reduce-scatter.9.cloned.1.call-start = ((), (), s32[]{:S(2)}) async-start(), calls=%async_computation.15 | async-start | bytes 207618048 | tf_op jit(solution)/shard_map/reduce_scatter | solution.py:82
  1499.8 22.6 slice-start
  1510.8 11.6 slice-start.1
  1522.4 10.4 copy-start.11
  1815.7 3012.0 %reduce-scatter.11.cloned.1.call-start = ((), (), s32[]{:S(2)}) async-start(), calls=%async_computation.16 | async-start | bytes 69206016 | tf_op jit(solution)/shard_map/reduce_scatter | solution.py:97
  1862.2 30.1 copy-start.23
  1892.3 8.1 copy-start.24
  1900.4 11.6 copy-start.4
  1900.4 11.5 copy-start.22
  1900.4 11.5 copy-start.34
  1900.4 11.5 copy-start.38
  1912.0 13.7 copy-start.42
  (13 other events, 39.4 us)
Sparse Core Ops, SparseCore 0:
  11.0 80.4 all-gather.17
  94.4 76.0 all-gather.15
  173.4 75.8 all-gather.11
  251.3 147.8 all-gather.19
  401.1 147.3 all-gather.13
  551.3 75.5 all-gather.21
  629.7 193.3 all-gather.25
  826.1 192.9 all-gather.23
  1022.0 192.9 all-gather.27
  1362.9 142.6 reduce-scatter.6
  1508.0 145.1 reduce-scatter.4
  1815.9 1599.2 reduce-scatter.8
  3418.1 1409.5 reduce-scatter.10
where the time goes:
time: 4840 us; the launch traced here: 4830 us
  waiting for transfers between devices  3820 us (79%)
  matrix products  572 us (12%)
  other arithmetic  260 us (5%)
  blocking collectives  104 us (2%)
  local copies, waits for them, and re-layouts  66.2 us (1%)
    reduce_scatter x1, waiting for transfers between devices, send_grads(): lax.psum_scatter(jnp.concatenate([contract_first(normed, attn_grads), con...  1440 us
    reduce_scatter x1, waiting for transfers between devices, send_grads(): lax.psum_scatter(down_total, ('dp', 'seq'), scatter_dimension=0, tiled=True)  1410 us
    all_gather x1, waiting for transfers between devices, on_device(): lax.all_gather(w_up, ('dp', 'seq'), axis=0, tiled=True)  186 us
    all_gather x1, waiting for transfers between devices, on_device(): lax.all_gather(w_gate, ('dp', 'seq'), axis=0, tiled=True)  169 us
    all_gather x1, waiting for transfers between devices, on_device(): lax.all_gather(w_down, ('dp', 'seq'), axis=0, tiled=True)  169 us
    dot_general x4, matrix products, contract_first(): lax.dot_general(left, right, (((0,), (0,)), ((), ())), preferred_element_...  135 us
    dot_general x7, matrix products, contract_last(): lax.dot_general(left, right, (((1,), (1,)), ((), ())), preferred_element_...  134 us
    concatenate x1, other arithmetic, send_grads(): jnp.concatenate([contract_first(normed, attn_grads), contract_first(atten...  131 us
  transfers between devices with their start and end apart: 13, of which 12 were waited for; matrix products, arithmetic and copies ran while one was open for 12% of the time, Pallas kernels for 0%

commit v1 on v0

v1 whole, which is shorter than its diff:
```python
import functools

import jax
import jax.numpy as jnp
from jax import lax
from jax.experimental import pallas as pl
from jax.experimental.pallas import tpu as pltpu
from jax.sharding import Mesh
from jax.sharding import PartitionSpec as P

HD = 64
NORM_EPS = 1e-05
ROPE_BASE = 130000.0
MASK_FILL = -1e30
LANES = 128
VMEM_BYTES = 56 * 1024 * 1024
F32 = jnp.float32
BF16 = jnp.bfloat16


def dot(left, right):
    return jnp.dot(left, right, preferred_element_type=F32)


def contract_last(left, right):
    return lax.dot_general(left, right, (((1,), (1,)), ((), ())), preferred_element_type=F32)


def contract_first(left, right):
    return lax.dot_general(left, right, (((0,), (0,)), ((), ())), preferred_element_type=F32)


def norm_scale(values):
    return lax.rsqrt(jnp.mean(values * values, axis=-1, keepdims=True) + NORM_EPS)


def norm_back(grad_normed, values, scale_rows, gain):
    unit = values * scale_rows
    scaled = grad_normed * gain
    grad_values = scale_rows * (scaled - unit * jnp.mean(scaled * unit, axis=-1, keepdims=True))
    return (grad_values, jnp.sum(grad_normed * unit, axis=0))


def fill_bias(doc_col, doc_row, bias, block):
    length = bias.shape[0]
    for start in range(0, length, block):
        rows = doc_col[start : start + block, :]
        columns = doc_row[...]
        key_pos = start + lax.broadcasted_iota(jnp.int32, (block, length), 0)
        query_pos = lax.broadcasted_iota(jnp.int32, (block, length), 1)
        same = (rows >> 1) == (columns >> 1)
        open_key = ((rows & 1) == 1) | (key_pos == query_pos)
        allowed = same & (key_pos <= query_pos) & open_key
        bias[start : start + block, :] = jnp.where(allowed, 0.0, MASK_FILL)


def partner(field):
    lane = lax.broadcasted_iota(jnp.int32, field.shape, 1)
    return jnp.where(
        (lane % HD) < HD // 2,
        pltpu.roll(field, LANES - HD // 2, 1),
        pltpu.roll(field, HD // 2, 1),
    )


def split_heads(rows):
    lane = lax.broadcasted_iota(jnp.int32, rows.shape, 1)
    zero = jnp.zeros_like(rows)
    return jnp.concatenate(
        [jnp.where(lane < HD, rows, zero), jnp.where(lane < HD, zero, rows)], axis=0
    )


def join_heads(stacked):
    half = stacked.shape[0] // 2
    lane = lax.broadcasted_iota(jnp.int32, (half, LANES), 1)
    return jnp.where(lane < HD, stacked[:half], stacked[half:])


def attend_kernel(
    block, doc_col, doc_row, cosine, sine, raw, mixed, rotated, log_total, bias
):
    length = bias.shape[0]

    @pl.when(pl.program_id(0) == 0)
    def _():
        fill_bias(doc_col, doc_row, bias, block)

    query = raw[:, 0:LANES]
    key = raw[:, LANES : 2 * LANES]
    scale = float(HD) ** (-0.5)
    query = ((query * cosine[...] + partner(query) * sine[...]) * scale).astype(BF16)
    key = (key * cosine[...] + partner(key) * sine[...]).astype(BF16)
    value = raw[:, 2 * LANES : 3 * LANES].astype(BF16)
    rotated[:, 0:LANES] = query
    rotated[:, LANES : 2 * LANES] = key
    rotated[:, 2 * LANES : 3 * LANES] = value
    value_t = value.T
    for start in range(0, length, block):
        stop = start + block
        stacked = split_heads(query[start:stop])
        scores = contract_last(key[:stop], stacked)
        hide = bias[:stop, start:stop]
        scores = scores + jnp.concatenate([hide, hide], axis=1)
        top = jnp.max(scores, axis=0, keepdims=True)
        weights = jnp.exp(scores - top)
        total = jnp.sum(weights, axis=0, keepdims=True)
        probs = (weights * (1.0 / total)).astype(BF16)
        out_t = dot(value_t[:, :stop], probs)
        mixed[start:stop, :] = join_heads(out_t.T).astype(BF16)
        log_total[0, :, 2 * start : 2 * stop] = top + jnp.log(total)


def attend_back_kernel(
    block, doc_col, doc_row, cosine, sine, rotated, grad_mixed, log_total, grads, bias, key_sum, value_sum
):
    length = bias.shape[0]

    @pl.when(pl.program_id(0) == 0)
    def _():
        fill_bias(doc_col, doc_row, bias, block)

    scale = float(HD) ** (-0.5)
    key = rotated[:, LANES : 2 * LANES]
    value = rotated[:, 2 * LANES : 3 * LANES]
    key_t = key.T
    for start in range(length - block, -1, -block):
        stop = start + block
        queries = split_heads(rotated[start:stop, 0:LANES])
        outs = split_heads(grad_mixed[start:stop, :])
        scores = contract_last(key[:stop], queries)
        hide = bias[:stop, start:stop]
        scores = scores + jnp.concatenate([hide, hide], axis=1)
        probs = jnp.exp(scores - log_total[0, :, 2 * start : 2 * stop])
        grad_probs = contract_last(value[:stop], outs)
        inner = jnp.sum(grad_probs * probs, axis=0, keepdims=True)
        grad_scores = (probs * (grad_probs - inner)).astype(BF16)
        key_part = dot(grad_scores, queries)
        value_part = dot(probs.astype(BF16), outs)
        if stop == length:
            key_sum[...] = key_part
            value_sum[...] = value_part
        else:
            key_sum[:stop, :] += key_part
            value_sum[:stop, :] += value_part
        grad_query = join_heads(dot(key_t[:, :stop], grad_scores).T) * scale
        turned = grad_query * cosine[start:stop, :] - partner(grad_query) * sine[start:stop, :]
        grads[start:stop, 0:LANES] = turned.astype(BF16)
    grad_key = key_sum[...]
    turned = grad_key * cosine[...] - partner(grad_key) * sine[...]
    grads[:, LANES : 2 * LANES] = turned.astype(BF16)
    grads[:, 2 * LANES : 3 * LANES] = value_sum[...].astype(BF16)


def attention_specs(length):
    whole = lambda shape: pl.BlockSpec(shape, lambda pair: (0, 0))
    columns = lambda width: pl.BlockSpec((length, width), lambda pair: (0, pair))
    totals = pl.BlockSpec((1, 1, 2 * length), lambda pair: (pair, 0, 0))
    shared = [whole((length, 1)), whole((1, length)), whole((length, LANES)), whole((length, LANES))]
    return (shared, columns, totals)


def attend(doc_row, cosine, sine, raw):
    length = raw.shape[0]
    pairs = raw.shape[1] // (3 * LANES)
    block = min(256, length)
    shared, columns, totals = attention_specs(length)
    work = pairs * 2 * length * (length + block) * LANES
    return pl.pallas_call(
        functools.partial(attend_kernel, block),
        grid=(pairs,),
        in_specs=shared + [columns(3 * LANES)],
        out_specs=[columns(LANES), columns(3 * LANES), totals],
        out_shape=[
            jax.ShapeDtypeStruct((length, pairs * LANES), BF16),
            jax.ShapeDtypeStruct((length, pairs * 3 * LANES), BF16),
            jax.ShapeDtypeStruct((pairs, 1, 2 * length), F32),
        ],
        scratch_shapes=[pltpu.VMEM((length, length), F32)],
        compiler_params=pltpu.CompilerParams(vmem_limit_bytes=VMEM_BYTES),
        cost_estimate=pl.CostEstimate(
            flops=4 * work, bytes_accessed=20 * length * pairs * LANES, transcendentals=work // LANES
        ),
        name="attend",
    )(doc_row[:, None], doc_row[None, :], cosine, sine, raw)


def attend_back(doc_row, cosine, sine, rotated, grad_mixed, log_total):
    length = rotated.shape[0]
    pairs = rotated.shape[1] // (3 * LANES)
    block = min(256, length)
    shared, columns, totals = attention_specs(length)
    work = pairs * 2 * length * (length + block) * LANES
    return pl.pallas_call(
        functools.partial(attend_back_kernel, block),
        grid=(pairs,),
        in_specs=shared + [columns(3 * LANES), columns(LANES), totals],
        out_specs=columns(3 * LANES),
        out_shape=jax.ShapeDtypeStruct((length, pairs * 3 * LANES), BF16),
        scratch_shapes=[
            pltpu.VMEM((length, length), F32),
            pltpu.VMEM((length, LANES), F32),
            pltpu.VMEM((length, LANES), F32),
        ],
        compiler_params=pltpu.CompilerParams(vmem_limit_bytes=VMEM_BYTES),
        cost_estimate=pl.CostEstimate(
            flops=10 * work, bytes_accessed=14 * length * pairs * LANES, transcendentals=work // LANES
        ),
        name="attend_back",
    )(doc_row[:, None], doc_row[None, :], cosine, sine, rotated, grad_mixed, log_total)


class Axis:
    def __init__(self, name, count):
        self.name = name
        self.count = count

    @property
    def place(self):
        return lax.axis_index(self.name)

    def swap(self, block):
        return lax.ppermute(block, self.name, [(0, 1), (1, 0)])

    def in_order(self, own, other):
        first = self.place == 0
        return jnp.stack([jnp.where(first, own, other), jnp.where(first, other, own)])

    def own(self, blocks):
        return lax.dynamic_index_in_dim(blocks, self.place, 0, keepdims=False)

    def other(self, blocks):
        return lax.dynamic_index_in_dim(blocks, 1 - self.place, 0, keepdims=False)

    def gather(self, block):
        if self.count == 1:
            return block[None]
        if self.count == 2:
            return self.in_order(block, self.swap(block))
        return lax.all_gather(block, self.name, axis=0, tiled=False)

    def exchange(self, blocks):
        if self.count == 1:
            return blocks
        if self.count == 2:
            return self.in_order(self.own(blocks), self.swap(self.other(blocks)))
        return lax.all_to_all(blocks, self.name, split_axis=0, concat_axis=0, tiled=True)

    def scatter(self, blocks):
        if self.count == 1:
            return blocks[0].astype(F32)
        if self.count == 2:
            received = self.swap(self.other(blocks).astype(BF16))
            return self.own(blocks).astype(F32) + received.astype(F32)
        return lax.psum_scatter(
            blocks.astype(BF16), self.name, scatter_dimension=0, tiled=False
        ).astype(F32)


class Line(Axis):
    def exchange(self, blocks):
        count, place = self.count, self.place
        pieces = [lax.dynamic_index_in_dim(blocks, place, 0, keepdims=False)]
        for shift in range(1, count):
            piece = lax.dynamic_index_in_dim(blocks, (place + shift) % count, 0, keepdims=False)
            pairs = [(i, (i + shift) % count) for i in range(count)]
            pieces.append(lax.ppermute(piece, self.name, pairs))
        turned = [pieces[-j % count] for j in range(count)]
        doubled = jnp.stack(turned + turned)
        return lax.dynamic_slice_in_dim(doubled, count - place, count, 0)

    def gather_rows(self, block, axis):
        return lax.all_gather(block, self.name, axis=axis, tiled=True)

    def scatter_rows(self, block, axis):
        return lax.psum_scatter(block, self.name, scatter_dimension=axis, tiled=True)


def on_device(
    sizes,
    inputs,
    cotangent,
    doc_ids,
    valid_mask,
    gain_attn,
    w_query,
    w_key,
    w_value,
    w_out,
    gain_mlp,
    w_gate,
    w_up,
    w_down,
):
    y_axis, x_axis, c_axis, z_axis, t_axis, line = sizes
    micro_count, _, tokens, width = inputs.shape
    rows = w_query.shape[0]
    hidden_units = w_gate.shape[1]
    planes = y_axis.count * x_axis.count
    cores, turns, depth = c_axis.count, t_axis.count, line.count
    part = tokens // (cores * turns)
    own_tokens = depth * part
    length = depth * tokens
    head_block = width // (planes * cores)
    pair_count = head_block // LANES
    hidden_block = hidden_units // (planes * cores)
    everyone = (y_axis.name, x_axis.name, c_axis.name) + line.name

    def to_sequences(block):
        pieces = block[:, 0].reshape(micro_count, cores, turns, part, width)
        pieces = c_axis.exchange(pieces.transpose(1, 0, 2, 3, 4))
        pieces = pieces.transpose(1, 0, 2, 3, 4).reshape(depth, part, width)
        return line.exchange(pieces).reshape(own_tokens, width)

    def from_sequences(block):
        pieces = line.exchange(block.reshape(depth, part, width))
        pieces = pieces.reshape(micro_count, cores, turns, part, width).transpose(1, 0, 2, 3, 4)
        pieces = c_axis.exchange(pieces).transpose(1, 0, 2, 3, 4)
        return pieces.reshape(micro_count, 1, tokens, width)

    def whole_sequence(block):
        pieces = c_axis.gather(t_axis.gather(block.reshape(depth, part, width)))
        return pieces.transpose(2, 0, 1, 3, 4).reshape(length, width)

    def own_share(total):
        pieces = total.reshape(depth, cores, turns, part, width).transpose(1, 2, 0, 3, 4)
        return t_axis.scatter(c_axis.scatter(pieces)).reshape(own_tokens, width)

    def to_group(block):
        return c_axis.gather(x_axis.gather(block)).reshape(-1, width)

    def from_group(total):
        pieces = total.reshape(cores, x_axis.count, own_tokens, width)
        return x_axis.scatter(c_axis.scatter(pieces))

    packed = lax.all_gather(
        doc_ids[:, 0] * 2 + valid_mask[:, 0], (c_axis.name,) + line.name, axis=0, tiled=False
    ).reshape(cores, depth, micro_count, tokens)
    gains = lax.all_gather(
        jnp.concatenate([gain_attn, gain_mlp])[None], everyone, axis=0, tiled=True
    )
    gains = gains.reshape(-1, 2, rows).transpose(1, 0, 2).reshape(2, width).astype(F32)

    own_in = to_sequences(inputs)

    joined = jnp.stack([w_query, w_key, w_value], axis=1)
    joined = joined.reshape(rows, 3, planes, cores, pair_count, LANES)
    joined = joined.transpose(3, 0, 2, 4, 1, 5).reshape(cores, rows, 3 * width // cores)
    joined = line.gather_rows(c_axis.exchange(joined), 1)
    w_qkv = x_axis.gather(y_axis.gather(joined)).transpose(1, 0, 2, 3, 4).reshape(width, -1)
    own_out = line.gather_rows(w_out, 0)
    own_out = x_axis.gather(y_axis.gather(own_out)).transpose(1, 0, 2, 3).reshape(-1, width)

    def hidden_columns(weight):
        pieces = weight.reshape(rows, y_axis.count, x_axis.count, cores, hidden_block)
        pieces = pieces.transpose(3, 2, 0, 1, 4).reshape(cores, x_axis.count, rows, -1)
        pieces = x_axis.exchange(c_axis.exchange(pieces).transpose(1, 0, 2, 3))
        pieces = line.gather_rows(pieces.reshape(x_axis.count * cores, rows, -1), 1)
        return y_axis.gather(pieces).reshape(width, -1)

    own_gate = hidden_columns(w_gate)
    own_up = hidden_columns(w_up)
    own_down = y_axis.gather(line.gather_rows(w_down, 0)).reshape(-1, width)
    own_cotangent = to_sequences(cotangent)
    group_cotangent = to_group(own_cotangent)

    share = planes // turns
    if turns > 1:
        turn = t_axis.place * share
        qkv_blocks = w_qkv.reshape(width, planes, -1)
        w_qkv = lax.dynamic_slice_in_dim(qkv_blocks, turn, share, 1).reshape(width, -1)
        out_blocks = own_out.reshape(planes, -1, width)
        own_out = lax.dynamic_slice_in_dim(out_blocks, turn, share, 0).reshape(-1, width)

    z_place = lax.axis_index(z_axis.name)
    doc_row = lax.dynamic_index_in_dim(packed, z_place % cores, 0, keepdims=False)
    doc_row = lax.dynamic_index_in_dim(doc_row, z_place // cores, 1, keepdims=False).reshape(length)
    document = doc_row >> 1
    before = jnp.sum((document[None, :] < document[:, None]).astype(jnp.int32), axis=1)
    positions = (jnp.arange(length, dtype=jnp.int32) - before).astype(F32)
    lane = jnp.arange(LANES, dtype=jnp.int32)
    exponent = (lane % (HD // 2)).astype(F32) * (2.0 / HD)
    angles = positions[:, None] * jnp.power(ROPE_BASE, -exponent)[None, :]
    cosine = jnp.cos(angles)
    sine = jnp.where((lane % HD) < HD // 2, -1.0, 1.0)[None, :] * jnp.sin(angles)

    all_in = whole_sequence(own_in).astype(F32)
    normed = (all_in * norm_scale(all_in) * gains[0]).astype(BF16)
    mixed, rotated, log_total = attend(doc_row, cosine, sine, dot(normed, w_qkv))
    hidden_in = own_in.astype(F32)
    middle = hidden_in + own_share(dot(mixed, own_out))

    scale_mid = norm_scale(middle)
    normed_mlp = to_group((middle * scale_mid * gains[1]).astype(BF16))
    gate_proj = dot(normed_mlp, own_gate)
    up_proj = dot(normed_mlp, own_up)
    sigmoid_gate = jax.nn.sigmoid(gate_proj)
    silu_gate = gate_proj * sigmoid_gate
    activated = (silu_gate * up_proj).astype(BF16)
    result = middle + from_group(dot(activated, own_down))
    output = from_sequences(result.astype(BF16))

    grad_activated = contract_last(group_cotangent, own_down)
    grad_gate = (
        grad_activated * up_proj * sigmoid_gate * (1.0 + gate_proj * (1.0 - sigmoid_gate))
    ).astype(BF16)
    grad_up = (grad_activated * silu_gate).astype(BF16)
    grad_normed_mlp = from_group(contract_last(grad_gate, own_gate) + contract_last(grad_up, own_up))
    grad_mid_norm, gain_mlp_term = norm_back(grad_normed_mlp, middle, scale_mid, gains[1])
    grad_middle = own_cotangent.astype(F32) + grad_mid_norm

    def scatter_hidden_rows(grad):
        half = y_axis.scatter(grad.astype(BF16).reshape(y_axis.count, -1, width))
        return line.scatter_rows(half.astype(BF16), 0)

    def scatter_hidden_columns(grad):
        half = y_axis.scatter(
            grad.astype(BF16).reshape(y_axis.count, x_axis.count * cores, depth, rows, -1)
        )
        half = half.astype(BF16).transpose(1, 0, 2, 3).reshape(depth * x_axis.count * cores * rows, -1)
        mine = line.scatter_rows(half, 0).reshape(x_axis.count, cores, rows, -1)
        mine = x_axis.exchange(mine).transpose(1, 0, 2, 3)
        mine = c_axis.exchange(mine).reshape(cores, x_axis.count, rows, y_axis.count, hidden_block)
        return mine.transpose(2, 3, 1, 0, 4).reshape(rows, hidden_units).astype(F32)

    grad_gate_shard = scatter_hidden_columns(contract_first(normed_mlp, grad_gate))
    grad_up_shard = scatter_hidden_columns(contract_first(normed_mlp, grad_up))
    grad_down_shard = scatter_hidden_rows(contract_first(activated, group_cotangent)).astype(F32)

    grad_branch = whole_sequence(grad_middle.astype(BF16))
    grad_mixed = contract_last(grad_branch, own_out).astype(BF16)
    grad_out = contract_first(mixed, grad_branch).astype(BF16)
    grad_raw = attend_back(doc_row, cosine, sine, rotated, grad_mixed, log_total)
    grad_normed = own_share(contract_last(grad_raw, w_qkv))
    grad_in_norm, gain_attn_term = norm_back(
        grad_normed, hidden_in, norm_scale(hidden_in), gains[0]
    )
    grad_input = from_sequences((grad_middle + grad_in_norm).astype(BF16))
    grad_qkv = contract_first(normed, grad_raw).astype(BF16)
    if turns > 1:
        blocks = grad_qkv.reshape(width, share, -1)
        blank = jnp.zeros((width, planes, blocks.shape[2]), BF16)
        grad_qkv = lax.dynamic_update_slice_in_dim(blank, blocks, turn, 1).reshape(width, -1)
        blocks = grad_out.reshape(share, -1, width)
        blank = jnp.zeros((planes, blocks.shape[1], width), BF16)
        grad_out = lax.dynamic_update_slice_in_dim(blank, blocks, turn, 0).reshape(-1, width)

    def scatter_planes(grad, trailing):
        pieces = grad.reshape((y_axis.count, x_axis.count) + trailing)
        pieces = x_axis.scatter(pieces.transpose((1, 0) + tuple(range(2, pieces.ndim))))
        return y_axis.scatter(pieces.astype(BF16)).astype(BF16)

    grad_out_shard = line.scatter_rows(scatter_planes(grad_out, (depth * rows, width)), 0)
    mine = scatter_planes(grad_qkv, (cores, depth, rows, 3 * width // cores))
    mine = mine.transpose(1, 0, 2, 3).reshape(depth * cores * rows, -1)
    mine = c_axis.exchange(line.scatter_rows(mine, 0).reshape(cores, rows, -1))
    mine = mine.reshape(cores, rows, planes, pair_count, 3, LANES).transpose(4, 1, 2, 0, 3, 5)
    mine = mine.reshape(3, rows, width).astype(F32)

    terms = jnp.stack([gain_attn_term, gain_mlp_term])
    for axis in (c_axis, x_axis, y_axis, z_axis, t_axis):
        if axis.count == 1:
            continue
        if axis.count == 2:
            terms = terms + axis.swap(terms)
        else:
            terms = lax.psum(terms, axis.name)
    rank = lax.axis_index(everyone)
    terms = lax.dynamic_slice_in_dim(terms, rank * rows, rows, 1)

    return (
        output,
        grad_input,
        terms[0],
        mine[0],
        mine[1],
        mine[2],
        grad_out_shard.astype(F32),
        terms[1],
        grad_gate_shard,
        grad_up_shard,
        grad_down_shard,
    )


def solution(mesh):
    dp, seq = mesh.shape["dp"], mesh.shape["seq"]
    names = ("y", "x", "c", "z", "t")

    def step(*arrays):
        micro_count = arrays[0].shape[0]
        turns = seq // (2 * micro_count)
        shape = (2, dp // 4, 2, seq // turns, turns)
        fine = Mesh(mesh.devices.reshape(shape), names)
        axes = [Axis(name, count) for name, count in zip(names, shape)]
        sizes = tuple(axes) + (Line(("z", "t"), seq),)
        row, shard = ("y", "x", "c"), ("y", "x", "c", "z", "t")
        tokens_at = P(None, row, ("z", "t"), None)
        ids_at = P(None, row, ("z", "t"))
        vector, matrix = P(shard), P(shard, None)
        return jax.shard_map(
            functools.partial(on_device, sizes),
            mesh=fine,
            in_specs=(tokens_at, tokens_at, ids_at, ids_at, vector)
            + (matrix,) * 4
            + (vector,)
            + (matrix,) * 3,
            out_specs=(tokens_at, tokens_at, vector)
            + (matrix,) * 4
            + (vector,)
            + (matrix,) * 3,
            check_vma=False,
        )(*arrays)

    return step
```

time: 4840 us -> 1860 us (0.38)
  waiting for transfers between devices: 3820 us -> 835 us
  matrix products: 572 us -> 298 us
  local copies, waits for them, and re-layouts: 66.2 us -> 178 us
  starting transfers between devices: 0.72 us -> 78.5 us
  blocking collectives: 104 us -> 180 us
  Pallas kernels: 0 us -> 67.8 us
  other arithmetic: 260 us -> 200 us
    reduce_scatter x4 -> x5, waiting for transfers between devices: 2900 us -> 0.05 us  [scatter_rows(): lax.psum_scatter(block, self.name, scatter_dimension=axis, tiled=True)]
    all_gather x9 -> x5, waiting for transfers between devices: 908 us -> 0.01 us  [gather_rows(): return lax.all_gather(block, self.name, axis=axis, tiled=True)]
    ppermute x0 -> x55, waiting for transfers between devices: none -> 834 us  [the longest x43 710 us: swap(): return lax.ppermute(block, self.name, [(0, 1), (1, 0)])]
    dot_general x19 -> x5, matrix products: 303 us -> 88 us  [dot(): return jnp.dot(left, right, preferred_element_type=F32)]
    concatenate x4 -> x0, other arithmetic: 135 us -> none  [the longest x1 131 us: send_grads(): jnp.concatenate([contract_first(normed, attn_grads), contract_first(atten...]
    psum x0 -> x1, blocking collectives: none -> 88.7 us  [on_device(): terms = lax.psum(terms, axis.name)]
    unnamed x2 -> x0, blocking collectives: 84.1 us -> none
    another operation x4 -> x38, other arithmetic: 18.9 us -> 99.7 us  [the longest x37 99.6 us: in_order(): jnp.stack([jnp.where(first, own, other), jnp.where(first, other, own)])]
  transfers between devices with their start and end apart: 13 -> 65, of which waited for: 12 -> 21; matrix products, arithmetic and copies ran while one was open for 12% -> 28% of each run, Pallas kernels for 0% -> 4%
where the time goes in v1:
time: 1860 us; the launch traced here: 1850 us
  waiting for transfers between devices  835 us (45%)
  matrix products  298 us (16%)
  other arithmetic  200 us (11%)
  blocking collectives  180 us (10%)
  local copies, waits for them, and re-layouts  178 us (10%)
  starting transfers between devices  78.5 us (4%)
  Pallas kernels  67.8 us (4%)
    ppermute x43, waiting for transfers between devices, swap(): return lax.ppermute(block, self.name, [(0, 1), (1, 0)])  710 us
    ppermute x12, waiting for transfers between devices, exchange(): pieces.append(lax.ppermute(piece, self.name, pairs))  124 us
    dot_general x5, matrix products, contract_last(): lax.dot_general(left, right, (((1,), (1,)), ((), ())), preferred_element_...  110 us
    another operation x37, other arithmetic, in_order(): jnp.stack([jnp.where(first, own, other), jnp.where(first, other, own)])  99.6 us
    dot_general x5, matrix products, contract_first(): lax.dot_general(left, right, (((0,), (0,)), ((), ())), preferred_element_...  99.4 us
    psum x1, blocking collectives, on_device(): terms = lax.psum(terms, axis.name)  88.7 us
    dot_general x5, matrix products, dot(): return jnp.dot(left, right, preferred_element_type=F32)  88 us
    all_gather x1, blocking collectives, on_device(): lax.all_gather(jnp.concatenate([gain_attn, gain_mlp])[None], everyone, ax...  68.3 us
  transfers between devices with their start and end apart: 65, of which 21 were waited for; matrix products, arithmetic and copies ran while one was open for 28% of the time, Pallas kernels for 4%

profile of v1, /device:TPU:0, one launch (start us, length us, event | category | flops | bytes accessed | tf_op | source)
XLA Modules:
  0.0 1852.9 jit_solution(15304133788798033784)
XLA Ops:
  26.8 12.2 collective-permute-done.17
  48.8 23.1 %all-gather = s32[16,1,256]{2,1,0:T(1,128)S(1)} all-gather(s32[2,1,256]{2,1,0:T(1,128)S(1)} %multiply_add_fusion.1), channel_id=2, replica_groups=mesh['y'=2,'x'=2,'c'=2,'z'=4,'t'=1] {'c','z','t'}, dimensions={0}, use_global_device_ids=true | all-gather | bytes 18432 | tf_op jit(solution)/shard_map/all_gather | solution.py:336
  72.2 68.3 %all-gather.2 = bf16[32,1,128]{2,1,0:T(2,128)(2,1)S(1)} all-gather(bf16[1,1,128]{2,1,0:T(2,128)(2,1)S(1)} %maximum_bitcast_fusion.7), channel_id=3, replica_groups=mesh['y'=2,'x'=2,'c'=2,'z'=4,'t'=1] {'y','x','c','z','t'}, dimensions={0}, use_global_device_ids=true | all-gather | bytes 8448 | tf_op jit(solution)/shard_map/all_gather | solution.py:339
  160.5 60.3 %collective-permute-done.1 = bf16[128,2048]{1,0:T(8,128)(2,1)S(1)} collective-permute-done((bf16[128,2048]{1,0:T(8,128)(2,1)}, bf16[128,2048]{1,0:T(8,128)(2,1)S(1)}, u32[]{:S(2)}, u32[]{:S(2)}) %collective-permute-start.1) | collective-permute-done | bytes 524320 | tf_op jit(solution)/shard_map/ppermute | solution.py:267
  239.6 63.3 %collective-permute-done.27 = bf16[128,2048]{1,0:T(8,128)(2,1)S(1)} collective-permute-done((bf16[128,2048]{1,0:T(8,128)(2,1)}, bf16[128,2048]{1,0:T(8,128)(2,1)S(1)}, u32[]{:S(2)}, u32[]{:S(2)}) %collective-permute-start.27) | collective-permute-done | bytes 524320 | tf_op jit(solution)/shard_map/ppermute | solution.py:267
  320.4 17.5 collective-permute-done.8
  349.9 141.6 %collective-permute-done.9 = bf16[2,256,2048]{2,1,0:T(8,128)(2,1)S(1)} collective-permute-done((bf16[2,256,2048]{2,1,0:T(8,128)(2,1)S(1)}, bf16[2,256,2048]{2,1,0:T(8,128)(2,1)S(1)}, u32[]{:S(2)}, u32[]{:S(2)}) %collective-permute-start.9) | collective-permute-done | bytes 2097184 | tf_op jit(solution)/shard_map/ppermute | solution.py:223
  503.7 15.5 fusion.74.raw
  519.2 29.0 %attend.1 = (bf16[1024,1024]{1,0:T(8,128)(2,1)}, bf16[1024,3072]{1,0:T(8,128)(2,1)}, f32[8,1,2048]{2,1,0:T(1,128)}) custom-call(s32[1024,1]{1,0:T(8,128)} %bitcast.647, s32[1,1024]{1,0:T(1,128)} %bitcast.659, f32[1024,128]{1,0:T(8,128)} %get-tuple-element.147.cosine, f32[1024,128]{1,0:T(8,128)} %get-tuple-element.146.sine, f32[1024,3072]{1,0:T(8,128)} %fusion.74.raw), custom_call_target="tpu_custom_call" | custom-call | flops 10737418240 | bytes 20971520 | tf_op jit(solution)/shard_map/attend/pallas_call | solution.py:169
  582.0 39.2 %collective-permute-done.11 = bf16[512,2048]{1,0:T(8,128)(2,1)} collective-permute-done((bf16[512,2048]{1,0:T(8,128)(2,1)}, bf16[512,2048]{1,0:T(8,128)(2,1)}, u32[]{:S(2)}, u32[]{:S(2)}) %collective-permute-start.11) | collective-permute-done | bytes 2097184 | tf_op jit(solution)/shard_map/ppermute | solution.py:223
  626.0 7.5 pad_maximum_fusion.4
  633.5 23.3 %collective-permute-done.19 = bf16[1024,2048]{1,0:T(8,128)(2,1)} collective-permute-done((bf16[1024,2048]{1,0:T(8,128)(2,1)}, bf16[1024,2048]{1,0:T(8,128)(2,1)}, u32[]{:S(2)}, u32[]{:S(2)}) %collective-permute-start.19) | collective-permute-done | bytes 4194336 | tf_op jit(solution)/shard_map/ppermute | solution.py:223
  662.6 7.5 pad_maximum_fusion.3
  670.2 76.5 %collective-permute-done.18 = bf16[4,256,2048]{2,1,0:T(8,128)(2,1)} collective-permute-done((bf16[4,256,2048]{2,1,0:T(8,128)(2,1)}, bf16[4,256,2048]{2,1,0:T(8,128)(2,1)}, u32[]{:S(2)}, u32[]{:S(2)}) %collective-permute-start.18) | collective-permute-done | bytes 4194336 | tf_op jit(solution)/shard_map/ppermute | solution.py:223
  752.5 7.6 pad_maximum_fusion.2
  760.0 76.1 %collective-permute-done.15 = bf16[4,256,2048]{2,1,0:T(8,128)(2,1)} collective-permute-done((bf16[4,256,2048]{2,1,0:T(8,128)(2,1)}, bf16[4,256,2048]{2,1,0:T(8,128)(2,1)}, u32[]{:S(2)}, u32[]{:S(2)}) %collective-permute-start.15) | collective-permute-done | bytes 4194336 | tf_op jit(solution)/shard_map/ppermute | solution.py:223
  842.1 7.6 pad_maximum_fusion.1
  854.9 7.7 pad_maximum_fusion
  862.6 24.3 %fusion.77 = f32[2048,2048]{1,0:T(8,128)} fusion(bf16[2048,2048]{1,0:T(8,128)(2,1)} %bitcast.615, bf16[2048,2048]{1,0:T(8,128)(2,1)} %bitcast.607), kind=kOutput, calls=%fused_computation.316 | convolution fusion | flops 17179869184 | bytes 33554432 | tf_op jit(solution)/shard_map/dot_general | solution.py:22
  886.9 20.6 %fusion.76 = f32[2048,2048]{1,0:T(8,128)} fusion(bf16[2048,2048]{1,0:T(8,128)(2,1)S(1)} %bitcast.618, bf16[2048,2048]{1,0:T(8,128)(2,1)S(1)} %bitcast.612), kind=kOutput, calls=%fused_computation.315 | convolution fusion | flops 17179869184 | bytes 33554432 | tf_op jit(solution)/shard_map/dot_general | solution.py:22
  907.5 37.0 %multiply_convert_fusion = (bf16[2048,2048]{1,0:T(8,128)(2,1)}, bf16[2048,2048]{1,0:T(8,128)(2,1)}, bf16[2048,2048]{1,0:T(8,128)(2,1)}) fusion(f32[2048,2048]{1,0:T(8,128)} %fusion.76, f32[2048,2048]{1,0:T(8,128)} %fusion.77, bf16[2048,2048]{1,0:T(8,128)(2,1)} %bitcast.603, bf16[2048,2048]{1,0:T(8,128)(2,1)} %bitcast.613), kind=kOutput, calls=%fused_computation | convolution fusion | flops 17242783744 | bytes 75497472 | tf_op jit(solution)/shard_map/dot_general | solution.py:26
  944.5 21.5 %fusion.78 = f32[2,2,512,2048]{3,2,1,0:T(8,128)S(1)} fusion(bf16[2,2,512,2048]{3,2,1,0:T(8,128)(2,1)} %bitcast.661, bf16[2048,2048,1,1]{1,0,3,2:T(8,128)(2,1)} %bitcast.614), kind=kOutput, calls=%fused_computation.317 | convolution fusion | flops 17179869184 | bytes 33554432 | tf_op jit(solution)/shard_map/dot_general | solution.py:22
  968.9 27.9 %convolution_convert_fusion.2 = bf16[2048,2048]{1,0:T(8,128)(2,1)} fusion(bf16[2048,2048]{1,0:T(8,128)(2,1)} %bitcast.616, bf16[2048,2048]{1,0:T(8,128)(2,1)} %get-tuple-element.63), kind=kOutput, calls=%fused_computation.34 | convolution fusion | flops 17184063488 | bytes 25165824 | tf_op jit(solution)/shard_map/dot_general | solution.py:30
  1005.1 23.7 %convolution_convert_fusion.3 = bf16[2048,2048]{1,0:T(8,128)(2,1)} fusion(bf16[2048,2048]{1,0:T(8,128)(2,1)} %bitcast.617, bf16[2048,2048]{1,0:T(8,128)(2,1)} %get-tuple-element.64), kind=kOutput, calls=%fused_computation.35 | convolution fusion | flops 17184063488 | bytes 25165824 | tf_op jit(solution)/shard_map/dot_general | solution.py:30
  1028.9 6.7 constant_dynamic-slice_fusion.3
  1038.3 58.9 %collective-permute-done.51 = bf16[4,4,64,2048]{3,2,0,1:T(8,128)(2,1)S(1)} collective-permute-done((bf16[4,4,64,2048]{3,2,0,1:T(8,128)(2,1)}, bf16[4,4,64,2048]{3,2,0,1:T(8,128)(2,1)S(1)}, u32[]{:S(2)}, u32[]{:S(2)}) %collective-permute-start.51) | collective-permute-done | bytes 4194336 | tf_op jit(solution)/shard_map/ppermute | solution.py:223
  1101.2 24.7 %fusion.79 = f32[2048,2048]{1,0:T(8,128)} fusion(bf16[2048,2048]{1,0:T(8,128)(2,1)} %get-tuple-element.64, bf16[2048,2048]{1,0:T(8,128)(2,1)} %bitcast.609), kind=kOutput, calls=%fused_computation.318 | convolution fusion | flops 17179869184 | bytes 33554432 | tf_op jit(solution)/shard_map/dot_general | solution.py:26
  1125.9 26.3 %convolution_add_fusion = f32[2048,2048]{1,0:T(8,128)} fusion(f32[2048,2048]{1,0:T(8,128)} %fusion.79, bf16[2048,2048]{1,0:T(8,128)(2,1)} %get-tuple-element.63, bf16[2048,2048]{1,0:T(8,128)(2,1)} %bitcast.608), kind=kOutput, calls=%fused_computation.9 | convolution fusion | flops 17184063488 | bytes 50331648 | tf_op jit(solution)/shard_map/dot_general | solution.py:26
  1152.2 6.2 fusion.12
  1158.4 27.5 %collective-permute-done.48 = bf16[4,4,64,2048]{3,2,0,1:T(8,128)(2,1)} collective-permute-done((bf16[4,4,64,2048]{3,2,0,1:T(8,128)(2,1)}, bf16[4,4,64,2048]{3,2,0,1:T(8,128)(2,1)}, u32[]{:S(2)}, u32[]{:S(2)}) %collective-permute-start.48) | collective-permute-done | bytes 4194336 | tf_op jit(solution)/shard_map/ppermute | solution.py:223
  1192.0 24.0 %convolution_convert_fusion.1 = bf16[2048,2048]{1,0:T(8,128)(2,1)} fusion(bf16[2048,2048]{1,0:T(8,128)(2,1)} %get-tuple-element.65, bf16[2048,2048]{1,0:T(8,128)(2,1)} %bitcast.604), kind=kOutput, calls=%fused_computation.33 | convolution fusion | flops 17184063488 | bytes 25165824 | tf_op jit(solution)/shard_map/dot_general | solution.py:30
  1223.9 10.8 bitcast_add_fusion.1
  1245.9 25.2 %collective-permute-done.33 = bf16[512,2048]{1,0:T(8,128)(2,1)S(1)} collective-permute-done((bf16[512,2048]{1,0:T(8,128)(2,1)S(1)}, bf16[512,2048]{1,0:T(8,128)(2,1)S(1)}, u32[]{:S(2)}, u32[]{:S(2)}) %collective-permute-start.33) | collective-permute-done | bytes 2097184 | tf_op jit(solution)/shard_map/ppermute | solution.py:223
  1272.5 41.1 %collective-permute-done.21 = bf16[512,2048]{1,0:T(8,128)(2,1)} collective-permute-done((bf16[512,2048]{1,0:T(8,128)(2,1)}, bf16[512,2048]{1,0:T(8,128)(2,1)}, u32[]{:S(2)}, u32[]{:S(2)}) %collective-permute-start.21) | collective-permute-done | bytes 2097184 | tf_op jit(solution)/shard_map/ppermute | solution.py:223
  1313.6 6.6 fusion.72
  1326.6 7.7 collective-permute-done.54
  1334.3 7.9 fusion.2
  1345.2 30.3 %collective-permute-start.24 = (bf16[128,2048]{1,0:T(8,128)(2,1)}, bf16[128,2048]{1,0:T(8,128)(2,1)S(1)}, u32[]{:S(2)}, u32[]{:S(2)}) collective-permute-start(bf16[128,2048]{1,0:T(8,128)(2,1)} %get-tuple-element.116), channel_id=1, source_target_pairs={{0,1},{1,2},{2,3},{3,0},{4,5},{5,6},{6,7},{7,4},{8,9},{9,10},{10,1... | collective-permute-start | bytes 1572872 | tf_op jit(solution)/shard_map/ppermute | solution.py:267
  1391.6 38.8 %attend_back.1 = bf16[1024,3072]{1,0:T(8,128)(2,1)} custom-call(s32[1024,1]{1,0:T(8,128)} %bitcast.648, s32[1,1024]{1,0:T(1,128)} %bitcast.660, f32[1024,128]{1,0:T(8,128)} %get-tuple-element.147.cosine, f32[1024,128]{1,0:T(8,128)} %get-tuple-element.146.sine, bf16[1024,3072]{1,0:T(8,128)(2,1)} %get-tuple-element.15.rotated, ...), custom_call_target="tpu_custom_call" | custom-call | flops 26843545600 | bytes 14680064 | tf_op jit(solution)/shard_map/attend_back/pallas_call | solution.py:194
  1430.4 18.7 %convolution_convert_fusion = bf16[2048,3072]{1,0:T(8,128)(2,1)} fusion(bf16[1024,2048]{1,0:T(8,128)(2,1)S(1)} %copy-done.34, bf16[1024,3072]{1,0:T(8,128)(2,1)} %attend_back.1), kind=kOutput, calls=%fused_computation.8 | convolution fusion | flops 12891193344 | bytes 23068672 | tf_op jit(solution)/shard_map/dot_general | solution.py:30
  1449.1 11.3 constant_dynamic-slice_fusion.5
  1477.5 16.7 fusion.80
  1498.5 99.2 %collective-permute-done.43 = bf16[2,2,4,64,3072]{4,3,1,2,0:T(8,128)(2,1)S(1)} collective-permute-done((bf16[2,2,4,64,3072]{4,3,1,2,0:T(8,128)(2,1)S(1)}, bf16[2,2,4,64,3072]{4,3,1,2,0:T(8,128)(2,1)S(1)}, u32[]{:S(2)}, u32[]{:S(2)}) %collective-permute-start.43) | collective-permute-done | bytes 6291488 | tf_op jit(solution)/shard_map/ppermute | solution.py:223
  1600.3 7.5 fusion.1
  1629.7 43.8 %collective-permute-done.44 = bf16[2,4,64,3072]{3,2,0,1:T(8,128)(2,1)S(1)} collective-permute-done((bf16[2,4,64,3072]{3,2,0,1:T(8,128)(2,1)S(1)}, bf16[2,4,64,3072]{3,2,0,1:T(8,128)(2,1)S(1)}, u32[]{:S(2)}, u32[]{:S(2)}) %collective-permute-start.44) | collective-permute-done | bytes 3145760 | tf_op jit(solution)/shard_map/ppermute | solution.py:223
  1689.2 88.7 %psum.7 = f32[2,2048]{1,0:T(2,128)S(1)} all-reduce(f32[2,2048]{1,0:T(2,128)S(1)} %add.372), channel_id=1, replica_groups=mesh['y'=2,'x'=2,'c'=2,'z'=4,'t'=1] {'z'}, use_global_device_ids=true, to_apply=%region_8.9 | all-reduce | flops 4096 | bytes 32768 | tf_op jit(solution)/shard_map/psum | solution.py:467
  1801.7 7.2 collective-permute-done.52
  1810.1 9.5 collective-permute-done.49
  (447 shorter events, 352.9 us)
Async XLA Ops:
  7.2 220.4 %all-gather.9.cloned.1.call-start = ((), (), s32[]{:S(2)}) async-start(), calls=%async_computation.5 | async-start | bytes 3932160 | tf_op jit(solution)/shard_map/all_gather | solution.py:273
  17.7 295.4 %all-gather.11.cloned.1.call-start = ((), (), s32[]{:S(2)}) async-start(), calls=%async_computation.6 | async-start | bytes 1310720 | tf_op jit(solution)/shard_map/all_gather | solution.py:273
  18.5 544.6 %all-gather.17.cloned.1.call-start = ((), (), s32[]{:S(2)}) async-start(), calls=%async_computation.9 | async-start | bytes 5242880 | tf_op jit(solution)/shard_map/all_gather | solution.py:273
  19.2 555.2 %all-gather.15.cloned.1.call-start = ((), (), s32[]{:S(2)}) async-start(), calls=%async_computation.8 | async-start | bytes 5242880 | tf_op jit(solution)/shard_map/all_gather | solution.py:273
  40.3 534.9 %all-gather.13.cloned.1.call-start = ((), (), s32[]{:S(2)}) async-start(), calls=%async_computation.7 | async-start | bytes 5242880 | tf_op jit(solution)/shard_map/all_gather | solution.py:273
  43.7 101.9 %collective-permute-start.13 = (bf16[2,64,2048]{2,1,0:T(8,128)(2,1)}, bf16[2,64,2048]{2,1,0:T(8,128)(2,1)}, u32[]{:S(2)}, u32[]{:S(2)}) collective-permute-start(bf16[2,64,2048]{2,1,0:T(8,128)(2,1)} %dynamic-slice_bitcast_fusion.21), channel_id=1, source_target_pairs={{0,4},{4,0},{1,5},{5,1},{2,6},{6,2},{3,7},{7,3},{8,12},{12,8},{9,1... | collective-permute-start | bytes 1572872 | tf_op jit(solution)/shard_map/ppermute | solution.py:223
  46.0 100.8 %collective-permute-start.26 = (bf16[2,1,128,2048]{3,2,0,1:T(8,128)(2,1)}, bf16[2,1,128,2048]{3,2,0,1:T(8,128)(2,1)S(1)}, u32[]{:S(2)}, u32[]{:S(2)}) collective-permute-start(bf16[2,1,128,2048]{3,2,0,1:T(8,128)(2,1)} %dynamic-slice_bitcast_fusion.5), channel_id=1, source_target_pairs={{0,4},{4,0},{1,5},{5,1},{2,6},{6,2},{3,7},{7,3},{8,12},{12,8},{9,1... | collective-permute-start | bytes 3145736 | tf_op jit(solution)/shard_map/ppermute | solution.py:223
  48.8 99.9 %collective-permute-start = (bf16[2,1,128,2048]{3,2,0,1:T(8,128)(2,1)}, bf16[2,1,128,2048]{3,2,0,1:T(8,128)(2,1)S(1)}, u32[]{:S(2)}, u32[]{:S(2)}) collective-permute-start(bf16[2,1,128,2048]{3,2,0,1:T(8,128)(2,1)} %dynamic-slice_bitcast_fusion.7), channel_id=1, source_target_pairs={{0,4},{4,0},{1,5},{5,1},{2,6},{6,2},{3,7},{7,3},{8,12},{12,8},{9,1... | collective-permute-start | bytes 3145736 | tf_op jit(solution)/shard_map/ppermute | solution.py:223
  152.0 78.0 %collective-permute-start.3 = (bf16[128,2048]{1,0:T(8,128)(2,1)}, bf16[128,2048]{1,0:T(8,128)(2,1)S(1)}, u32[]{:S(2)}, u32[]{:S(2)}) collective-permute-start(bf16[128,2048]{1,0:T(8,128)(2,1)} %get-tuple-element.122), channel_id=1, source_target_pairs={{0,1},{1,2},{2,3},{3,0},{4,5},{5,6},{6,7},{7,4},{8,9},{9,10},{10,1... | collective-permute-start | bytes 1572872 | tf_op jit(solution)/shard_map/ppermute | solution.py:267
  152.0 75.6 %collective-permute-start.2 = (bf16[128,2048]{1,0:T(8,128)(2,1)}, bf16[128,2048]{1,0:T(8,128)(2,1)}, u32[]{:S(2)}, u32[]{:S(2)}) collective-permute-start(bf16[128,2048]{1,0:T(8,128)(2,1)} %get-tuple-element.124), channel_id=1, source_target_pairs={{0,2},{1,3},{2,0},{3,1},{4,6},{5,7},{6,4},{7,5},{8,10},{9,11},{10,... | collective-permute-start | bytes 1572872 | tf_op jit(solution)/shard_map/ppermute | solution.py:267
  152.0 68.8 %collective-permute-start.1 = (bf16[128,2048]{1,0:T(8,128)(2,1)}, bf16[128,2048]{1,0:T(8,128)(2,1)S(1)}, u32[]{:S(2)}, u32[]{:S(2)}) collective-permute-start(bf16[128,2048]{1,0:T(8,128)(2,1)} %get-tuple-element.125), channel_id=1, source_target_pairs={{0,3},{1,0},{2,1},{3,2},{4,7},{5,4},{6,5},{7,6},{8,11},{9,8},{10,9... | collective-permute-start | bytes 1572872 | tf_op jit(solution)/shard_map/ppermute | solution.py:267
  157.3 154.0 %collective-permute-start.29 = (bf16[128,2048]{1,0:T(8,128)(2,1)}, bf16[128,2048]{1,0:T(8,128)(2,1)}, u32[]{:S(2)}, u32[]{:S(2)}) collective-permute-start(bf16[128,2048]{1,0:T(8,128)(2,1)} %get-tuple-element.112), channel_id=1, source_target_pairs={{0,1},{1,2},{2,3},{3,0},{4,5},{5,6},{6,7},{7,4},{8,9},{9,10},{10,1... | collective-permute-start | bytes 1572872 | tf_op jit(solution)/shard_map/ppermute | solution.py:267
  157.8 151.5 %collective-permute-start.28 = (bf16[128,2048]{1,0:T(8,128)(2,1)}, bf16[128,2048]{1,0:T(8,128)(2,1)}, u32[]{:S(2)}, u32[]{:S(2)}) collective-permute-start(bf16[128,2048]{1,0:T(8,128)(2,1)} %get-tuple-element.114), channel_id=1, source_target_pairs={{0,2},{1,3},{2,0},{3,1},{4,6},{5,7},{6,4},{7,5},{8,10},{9,11},{10,... | collective-permute-start | bytes 1572872 | tf_op jit(solution)/shard_map/ppermute | solution.py:267
  160.4 1631.5 %reduce-scatter.12.cloned.1.call-start = ((), (), s32[]{:S(2)}) async-start(), calls=%async_computation.13 | async-start | bytes 5242880 | tf_op jit(solution)/shard_map/reduce_scatter | solution.py:276
  221.6 81.3 %collective-permute-start.27 = (bf16[128,2048]{1,0:T(8,128)(2,1)}, bf16[128,2048]{1,0:T(8,128)(2,1)S(1)}, u32[]{:S(2)}, u32[]{:S(2)}) collective-permute-start(bf16[128,2048]{1,0:T(8,128)(2,1)} %get-tuple-element.115), channel_id=1, source_target_pairs={{0,3},{1,0},{2,1},{3,2},{4,7},{5,4},{6,5},{7,6},{8,11},{9,8},{10,9... | collective-permute-start | bytes 1572872 | tf_op jit(solution)/shard_map/ppermute | solution.py:267
  227.6 76.2 %collective-permute-start.6 = (bf16[2,256,3072]{2,1,0:T(8,128)(2,1)}, bf16[2,256,3072]{2,1,0:T(8,128)(2,1)S(1)}, u32[]{:S(2)}, u32[]{:S(2)}) collective-permute-start(bf16[2,256,3072]{2,1,0:T(8,128)(2,1)} %all-gather.9.cloned.1.call-done), channel_id=1, source_target_pairs={{0,16},{16,0},{1,17},{17,1},{2,18},{18,2},{3,19},{19,3},{4,20},{20... | collective-permute-start | bytes 9437192 | tf_op jit(solution)/shard_map/ppermute | solution.py:223
  239.6 105.8 %collective-permute-start.4 = (bf16[1,4,128,2048]{3,2,1,0:T(8,128)(2,1)}, bf16[1,4,128,2048]{3,2,1,0:T(8,128)(2,1)}, u32[]{:S(2)}, u32[]{:S(2)}) collective-permute-start(bf16[1,4,128,2048]{3,2,1,0:T(8,128)(2,1)} %dynamic-slice_bitcast_fusion.8), channel_id=1, source_target_pairs={{0,4},{4,0},{1,5},{5,1},{2,6},{6,2},{3,7},{7,3},{8,12},{12,8},{9,1... | collective-permute-start | bytes 6291464 | tf_op jit(solution)/shard_map/ppermute | solution.py:223
  307.9 186.7 %collective-permute-start.7 = (bf16[2,2,256,3072]{3,2,1,0:T(8,128)(2,1)}, bf16[2,2,256,3072]{3,2,1,0:T(8,128)(2,1)}, u32[]{:S(2)}, u32[]{:S(2)}) collective-permute-start(bf16[2,2,256,3072]{3,2,1,0:T(8,128)(2,1)} %pad_maximum_fusion.5), channel_id=1, source_target_pairs={{0,8},{8,0},{1,9},{9,1},{2,10},{10,2},{3,11},{11,3},{4,12},{12,4},... | collective-permute-start | bytes 18874376 | tf_op jit(solution)/shard_map/ppermute | solution.py:223
  339.5 152.0 %collective-permute-start.9 = (bf16[2,256,2048]{2,1,0:T(8,128)(2,1)S(1)}, bf16[2,256,2048]{2,1,0:T(8,128)(2,1)S(1)}, u32[]{:S(2)}, u32[]{:S(2)}) collective-permute-start(bf16[2,256,2048]{2,1,0:T(8,128)(2,1)S(1)} %pad_maximum_fusion.9), channel_id=1, source_target_pairs={{0,8},{8,0},{1,9},{9,1},{2,10},{10,2},{3,11},{11,3},{4,12},{12,4},... | collective-permute-start | bytes 6291464 | tf_op jit(solution)/shard_map/ppermute | solution.py:223
  344.2 214.2 %collective-permute-start.30 = (bf16[512,2048]{1,0:T(8,128)(2,1)S(1)}, bf16[512,2048]{1,0:T(8,128)(2,1)}, u32[]{:S(2)}, u32[]{:S(2)}) collective-permute-start(bf16[512,2048]{1,0:T(8,128)(2,1)S(1)} %bitcast.580), channel_id=1, source_target_pairs={{0,8},{8,0},{1,9},{9,1},{2,10},{10,2},{3,11},{11,3},{4,12},{12,4},... | collective-permute-start | bytes 6291464 | tf_op jit(solution)/shard_map/ppermute | solution.py:223
  563.1 93.7 %collective-permute-start.19 = (bf16[1024,2048]{1,0:T(8,128)(2,1)}, bf16[1024,2048]{1,0:T(8,128)(2,1)}, u32[]{:S(2)}, u32[]{:S(2)}) collective-permute-start(bf16[1024,2048]{1,0:T(8,128)(2,1)} %all-gather.17.cloned.1.call-done), channel_id=1, source_target_pairs={{0,16},{16,0},{1,17},{17,1},{2,18},{18,2},{3,19},{19,3},{4,20},{20... | collective-permute-start | bytes 12582920 | tf_op jit(solution)/shard_map/ppermute | solution.py:223
  574.4 172.3 %collective-permute-start.18 = (bf16[4,256,2048]{2,1,0:T(8,128)(2,1)}, bf16[4,256,2048]{2,1,0:T(8,128)(2,1)}, u32[]{:S(2)}, u32[]{:S(2)}) collective-permute-start(bf16[4,256,2048]{2,1,0:T(8,128)(2,1)} %all-gather.15.cloned.1.call-done), channel_id=1, source_target_pairs={{0,16},{16,0},{1,17},{17,1},{2,18},{18,2},{3,19},{19,3},{4,20},{20... | collective-permute-start | bytes 12582920 | tf_op jit(solution)/shard_map/ppermute | solution.py:223
  575.2 261.0 %collective-permute-start.15 = (bf16[4,256,2048]{2,1,0:T(8,128)(2,1)}, bf16[4,256,2048]{2,1,0:T(8,128)(2,1)}, u32[]{:S(2)}, u32[]{:S(2)}) collective-permute-start(bf16[4,256,2048]{2,1,0:T(8,128)(2,1)} %all-gather.13.cloned.1.call-done), channel_id=1, source_target_pairs={{0,16},{16,0},{1,17},{17,1},{2,18},{18,2},{3,19},{19,3},{4,20},{20... | collective-permute-start | bytes 12582920 | tf_op jit(solution)/shard_map/ppermute | solution.py:223
  626.0 223.7 %collective-permute-start.12 = (bf16[2,512,2048]{2,1,0:T(8,128)(2,1)}, bf16[2,512,2048]{2,1,0:T(8,128)(2,1)}, u32[]{:S(2)}, u32[]{:S(2)}) collective-permute-start(bf16[2,512,2048]{2,1,0:T(8,128)(2,1)} %pad_maximum_fusion.7), channel_id=1, source_target_pairs={{0,4},{4,0},{1,5},{5,1},{2,6},{6,2},{3,7},{7,3},{8,12},{12,8},{9,1... | collective-permute-start | bytes 12582920 | tf_op jit(solution)/shard_map/ppermute | solution.py:223
  968.9 255.0 %collective-permute-start.20 = (bf16[2,512,2048]{2,1,0:T(8,128)(2,1)}, bf16[2,512,2048]{2,1,0:T(8,128)(2,1)}, u32[]{:S(2)}, u32[]{:S(2)}) collective-permute-start(bf16[2,512,2048]{2,1,0:T(8,128)(2,1)} %fusion.11), channel_id=1, source_target_pairs={{0,4},{4,0},{1,5},{5,1},{2,6},{6,2},{3,7},{7,3},{8,12},{12,8},{9,1... | collective-permute-start | bytes 12582920 | tf_op jit(solution)/shard_map/ppermute | solution.py:223
  1003.5 93.7 %collective-permute-start.51 = (bf16[4,4,64,2048]{3,2,0,1:T(8,128)(2,1)}, bf16[4,4,64,2048]{3,2,0,1:T(8,128)(2,1)S(1)}, u32[]{:S(2)}, u32[]{:S(2)}) collective-permute-start(bf16[4,4,64,2048]{3,2,0,1:T(8,128)(2,1)} %bitcast.574), channel_id=1, source_target_pairs={{0,16},{16,0},{1,17},{17,1},{2,18},{18,2},{3,19},{19,3},{4,20},{20... | collective-permute-start | bytes 12582920 | tf_op jit(solution)/shard_map/ppermute | solution.py:223
  1037.9 147.9 %collective-permute-start.48 = (bf16[4,4,64,2048]{3,2,0,1:T(8,128)(2,1)}, bf16[4,4,64,2048]{3,2,0,1:T(8,128)(2,1)}, u32[]{:S(2)}, u32[]{:S(2)}) collective-permute-start(bf16[4,4,64,2048]{3,2,0,1:T(8,128)(2,1)} %bitcast.575), channel_id=1, source_target_pairs={{0,16},{16,0},{1,17},{17,1},{2,18},{18,2},{3,19},{19,3},{4,20},{20... | collective-permute-start | bytes 12582920 | tf_op jit(solution)/shard_map/ppermute | solution.py:223
  1101.1 695.2 %reduce-scatter.10.cloned.1.call-start = ((), (), s32[]{:S(2)}) async-start(), calls=%async_computation.12 | async-start | bytes 5242880 | tf_op jit(solution)/shard_map/reduce_scatter | solution.py:276
  1158.4 57.6 %collective-permute-start.32 = (bf16[2,512,2048]{2,1,0:T(8,128)(2,1)}, bf16[2,512,2048]{2,1,0:T(8,128)(2,1)}, u32[]{:S(2)}, u32[]{:S(2)}) collective-permute-start(bf16[2,512,2048]{2,1,0:T(8,128)(2,1)} %fusion.12), channel_id=1, source_target_pairs={{0,4},{4,0},{1,5},{5,1},{2,6},{6,2},{3,7},{7,3},{8,12},{12,8},{9,1... | collective-permute-start | bytes 12582920 | tf_op jit(solution)/shard_map/ppermute | solution.py:223
  1191.9 607.0 %reduce-scatter.14.cloned.1.call-start = ((), (), s32[]{:S(2)}) async-start(), calls=%async_computation.14 | async-start | bytes 5242880 | tf_op jit(solution)/shard_map/reduce_scatter | solution.py:276
  1238.8 74.7 %collective-permute-start.21 = (bf16[512,2048]{1,0:T(8,128)(2,1)}, bf16[512,2048]{1,0:T(8,128)(2,1)}, u32[]{:S(2)}, u32[]{:S(2)}) collective-permute-start(bf16[512,2048]{1,0:T(8,128)(2,1)} %fusion.27), channel_id=1, source_target_pairs={{0,8},{8,0},{1,9},{9,1},{2,10},{10,2},{3,11},{11,3},{4,12},{12,4},... | collective-permute-start | bytes 6291464 | tf_op jit(solution)/shard_map/ppermute | solution.py:223
  1244.0 90.3 %collective-permute-start.54 = (bf16[1024,2048]{1,0:T(8,128)(2,1)}, bf16[1024,2048]{1,0:T(8,128)(2,1)}, u32[]{:S(2)}, u32[]{:S(2)}) collective-permute-start(bf16[1024,2048]{1,0:T(8,128)(2,1)} %dynamic-slice_bitcast_fusion), channel_id=1, source_target_pairs={{0,16},{16,0},{1,17},{17,1},{2,18},{18,2},{3,19},{19,3},{4,20},{20... | collective-permute-start | bytes 12582920 | tf_op jit(solution)/shard_map/ppermute | solution.py:223
  1320.2 59.4 %collective-permute-start.34 = (bf16[1,4,128,2048]{3,2,1,0:T(8,128)(2,1)}, bf16[1,4,128,2048]{3,2,1,0:T(8,128)(2,1)}, u32[]{:S(2)}, u32[]{:S(2)}) collective-permute-start(bf16[1,4,128,2048]{3,2,1,0:T(8,128)(2,1)} %bitcast.621), channel_id=1, source_target_pairs={{0,4},{4,0},{1,5},{5,1},{2,6},{6,2},{3,7},{7,3},{8,12},{12,8},{9,1... | collective-permute-start | bytes 6291464 | tf_op jit(solution)/shard_map/ppermute | solution.py:223
  1342.2 477.7 %reduce-scatter.6.cloned.1.call-start = ((), (), s32[]{:S(2)}) async-start(), calls=%async_computation.10 | async-start | bytes 3932160 | tf_op jit(solution)/shard_map/reduce_scatter | solution.py:276
  1345.2 122.8 %collective-permute-start.24 = (bf16[128,2048]{1,0:T(8,128)(2,1)}, bf16[128,2048]{1,0:T(8,128)(2,1)S(1)}, u32[]{:S(2)}, u32[]{:S(2)}) collective-permute-start(bf16[128,2048]{1,0:T(8,128)(2,1)} %get-tuple-element.116), channel_id=1, source_target_pairs={{0,1},{1,2},{2,3},{3,0},{4,5},{5,6},{6,7},{7,4},{8,9},{9,10},{10,1... | collective-permute-start | bytes 1572872 | tf_op jit(solution)/shard_map/ppermute | solution.py:267
  1375.5 91.6 %collective-permute-start.23 = (bf16[128,2048]{1,0:T(8,128)(2,1)}, bf16[128,2048]{1,0:T(8,128)(2,1)S(1)}, u32[]{:S(2)}, u32[]{:S(2)}) collective-permute-start(bf16[128,2048]{1,0:T(8,128)(2,1)} %get-tuple-element.118), channel_id=1, source_target_pairs={{0,2},{1,3},{2,0},{3,1},{4,6},{5,7},{6,4},{7,5},{8,10},{9,11},{10,... | collective-permute-start | bytes 1572872 | tf_op jit(solution)/shard_map/ppermute | solution.py:267
  1376.7 88.5 %collective-permute-start.22 = (bf16[128,2048]{1,0:T(8,128)(2,1)}, bf16[128,2048]{1,0:T(8,128)(2,1)}, u32[]{:S(2)}, u32[]{:S(2)}) collective-permute-start(bf16[128,2048]{1,0:T(8,128)(2,1)} %get-tuple-element.119), channel_id=1, source_target_pairs={{0,3},{1,0},{2,1},{3,2},{4,7},{5,4},{6,5},{7,6},{8,11},{9,8},{10,9... | collective-permute-start | bytes 1572872 | tf_op jit(solution)/shard_map/ppermute | solution.py:267
  1463.8 133.9 %collective-permute-start.43 = (bf16[2,2,4,64,3072]{4,3,1,2,0:T(8,128)(2,1)S(1)}, bf16[2,2,4,64,3072]{4,3,1,2,0:T(8,128)(2,1)S(1)}, u32[]{:S(2)}, u32[]{:S(2)}) collective-permute-start(bf16[2,2,4,64,3072]{4,3,1,2,0:T(8,128)(2,1)S(1)} %bitcast.623), channel_id=1, source_target_pairs={{0,8},{8,0},{1,9},{9,1},{2,10},{10,2},{3,11},{11,3},{4,12},{12,4},... | collective-permute-start | bytes 18874376 | tf_op jit(solution)/shard_map/ppermute | solution.py:223
  1477.4 132.3 %collective-permute-start.25 = (bf16[2,1,128,2048]{3,2,0,1:T(8,128)(2,1)}, bf16[2,1,128,2048]{3,2,0,1:T(8,128)(2,1)}, u32[]{:S(2)}, u32[]{:S(2)}) collective-permute-start(bf16[2,1,128,2048]{3,2,0,1:T(8,128)(2,1)} %dynamic-slice_bitcast_fusion.6), channel_id=1, source_target_pairs={{0,4},{4,0},{1,5},{5,1},{2,6},{6,2},{3,7},{7,3},{8,12},{12,8},{9,1... | collective-permute-start | bytes 3145736 | tf_op jit(solution)/shard_map/ppermute | solution.py:223
  1498.0 123.0 %collective-permute-start.35 = (bf16[1,4,128,2048]{3,2,1,0:T(8,128)(2,1)}, bf16[1,4,128,2048]{3,2,1,0:T(8,128)(2,1)}, u32[]{:S(2)}, u32[]{:S(2)}) collective-permute-start(bf16[1,4,128,2048]{3,2,1,0:T(8,128)(2,1)} %fusion.29), channel_id=1, source_target_pairs={{0,4},{4,0},{1,5},{5,1},{2,6},{6,2},{3,7},{7,3},{8,12},{12,8},{9,1... | collective-permute-start | bytes 6291464 | tf_op jit(solution)/shard_map/ppermute | solution.py:223
  1608.0 65.5 %collective-permute-start.44 = (bf16[2,4,64,3072]{3,2,0,1:T(8,128)(2,1)S(1)}, bf16[2,4,64,3072]{3,2,0,1:T(8,128)(2,1)S(1)}, u32[]{:S(2)}, u32[]{:S(2)}) collective-permute-start(bf16[2,4,64,3072]{3,2,0,1:T(8,128)(2,1)S(1)} %dynamic-slice_bitcast_fusion.1), channel_id=1, source_target_pairs={{0,16},{16,0},{1,17},{17,1},{2,18},{18,2},{3,19},{19,3},{4,20},{20... | collective-permute-start | bytes 9437192 | tf_op jit(solution)/shard_map/ppermute | solution.py:223
  1619.7 62.4 %collective-permute-start.46 = (bf16[2,256,2048]{2,1,0:T(8,128)(2,1)}, bf16[2,256,2048]{2,1,0:T(8,128)(2,1)}, u32[]{:S(2)}, u32[]{:S(2)}) collective-permute-start(bf16[2,256,2048]{2,1,0:T(8,128)(2,1)} %dynamic-slice_bitcast_fusion.2), channel_id=1, source_target_pairs={{0,8},{8,0},{1,9},{9,1},{2,10},{10,2},{3,11},{11,3},{4,12},{12,4},... | collective-permute-start | bytes 6291464 | tf_op jit(solution)/shard_map/ppermute | solution.py:223
  1627.2 54.1 %collective-permute-start.40 = (f32[2,2048]{1,0:T(2,128)S(1)}, f32[2,2048]{1,0:T(2,128)S(1)}, u32[]{:S(2)}, u32[]{:S(2)}) collective-permute-start(f32[2,2048]{1,0:T(2,128)S(1)} %pad_maximum_fusion.14), channel_id=1, source_target_pairs={{0,4},{4,0},{1,5},{5,1},{2,6},{6,2},{3,7},{7,3},{8,12},{12,8},{9,1... | collective-permute-start | bytes 49160 | tf_op jit(solution)/shard_map/ppermute | solution.py:223
  1676.5 160.2 %reduce-scatter.8.cloned.1.call-start = ((), (), s32[]{:S(2)}) async-start(), calls=%async_computation.11 | async-start | bytes 1310720 | tf_op jit(solution)/shard_map/reduce_scatter | solution.py:276
  1679.4 99.3 %collective-permute-start.37 = (bf16[128,2048]{1,0:T(8,128)(2,1)}, bf16[128,2048]{1,0:T(8,128)(2,1)S(1)}, u32[]{:S(2)}, u32[]{:S(2)}) collective-permute-start(bf16[128,2048]{1,0:T(8,128)(2,1)} %get-tuple-element.110), channel_id=1, source_target_pairs={{0,2},{1,3},{2,0},{3,1},{4,6},{5,7},{6,4},{7,5},{8,10},{9,11},{10,... | collective-permute-start | bytes 1572872 | tf_op jit(solution)/shard_map/ppermute | solution.py:267
  1679.4 98.5 %collective-permute-start.36 = (bf16[128,2048]{1,0:T(8,128)(2,1)}, bf16[128,2048]{1,0:T(8,128)(2,1)S(1)}, u32[]{:S(2)}, u32[]{:S(2)}) collective-permute-start(bf16[128,2048]{1,0:T(8,128)(2,1)} %get-tuple-element.111), channel_id=1, source_target_pairs={{0,3},{1,0},{2,1},{3,2},{4,7},{5,4},{6,5},{7,6},{8,11},{9,8},{10,9... | collective-permute-start | bytes 1572872 | tf_op jit(solution)/shard_map/ppermute | solution.py:267
  1687.9 101.4 %collective-permute-start.47 = (bf16[256,2048]{1,0:T(8,128)(2,1)}, bf16[256,2048]{1,0:T(8,128)(2,1)}, u32[]{:S(2)}, u32[]{:S(2)}) collective-permute-start(bf16[256,2048]{1,0:T(8,128)(2,1)} %dynamic-slice_bitcast_fusion.3), channel_id=1, source_target_pairs={{0,16},{16,0},{1,17},{17,1},{2,18},{18,2},{3,19},{19,3},{4,20},{20... | collective-permute-start | bytes 3145736 | tf_op jit(solution)/shard_map/ppermute | solution.py:223
  1688.5 91.1 %collective-permute-start.38 = (bf16[128,2048]{1,0:T(8,128)(2,1)}, bf16[128,2048]{1,0:T(8,128)(2,1)}, u32[]{:S(2)}, u32[]{:S(2)}) collective-permute-start(bf16[128,2048]{1,0:T(8,128)(2,1)} %get-tuple-element.108), channel_id=1, source_target_pairs={{0,1},{1,2},{2,3},{3,0},{4,5},{5,6},{6,7},{7,4},{8,9},{9,10},{10,1... | collective-permute-start | bytes 1572872 | tf_op jit(solution)/shard_map/ppermute | solution.py:267
  (82 other events, 1840.6 us)
Sparse Core Ops, SparseCore 0:
  17.9 66.3 all-gather.8
  85.8 26.7 all-gather.10
  114.2 146.1 all-gather.16
  261.8 89.8 all-gather.14
  353.0 79.3 all-gather.12
  1101.2 105.6 reduce-scatter.11
  1209.4 88.3 reduce-scatter.9
  1342.4 138.3 reduce-scatter.13
  1676.6 87.9 reduce-scatter.5
  1792.0 24.9 reduce-scatter.7
